TPU v7x, 128 devices: a whole 4x4x4 slice. The times are simulated.
128 devices in a mesh: dp: 4 (over x_lo, core), ctx: 32 (over z, y, x_hi).
Axes of the slice: x: 4 (x_hi: 2, x_lo: 2; x = x_hi * 2 + x_lo), y: 4, z: 4, core: 2. Of those that a mesh axis runs over, the one named last changes fastest.
Arguments:
- queries: bfloat16 [32768, 4096], P(('dp', 'ctx')), may hold values from -6 to 6
- keys: bfloat16 [32768, 512], P(('dp', 'ctx')), may hold values from -6 to 6
- values: bfloat16 [32768, 512], P(('dp', 'ctx')), may hold values from -6 to 6
- d_out: bfloat16 [4, 8192, 4096], P('dp', 'ctx'), may hold values from -6 to 6
- doc_ids: int32 [4, 8192], P('dp'), may hold values from 0 to 15, never falling along the last dimension, each value on 1 to 1024 neighbouring positions
- send_order: int32 [128, 256], P(('dp', 'ctx')), may hold values from 0 to 255, each once within a row
- place: int32 [128, 256], P(('dp', 'ctx')), may hold values from 0 to 255, each once within a row
Outputs:
- attended: bfloat16 [4, 8192, 4096], P('dp', 'ctx')
- grad_queries: bfloat16 [4, 8192, 4096], P('dp', 'ctx')
- grad_keys: bfloat16 [4, 8192, 512], P('dp', 'ctx')
- grad_values: bfloat16 [4, 8192, 512], P('dp', 'ctx')
Inputs may be any that keep to these rules, and one draw needn't show every extreme that they name: `doc_ids`: within each sequence the numbers never fall, every number from 0 to 15 is used, each document holds 1 to 1024 positions and one holds exactly 1024. `send_order`: each row is a permutation of 0 to 255. `place`: each row is a permutation of 0 to 255.
All inputs are finite; a program needn't handle non-finite values.
Results may differ from a plain program's by a relative error of at most 0.04.
Values may be sent and summed in bfloat16 or wider, within the bound.
No kernel may reach another device: no remote copies, remote signals or barrier semaphores. Data moves between devices by JAX's collectives and lax.ppermute only.
A program may use at most 192 MiB of HBM per device.

v0:
```python
import functools
import math

import jax
import jax.numpy as jnp
from jax import lax
from jax.experimental import pallas as pl
from jax.experimental.pallas import tpu as pltpu
from jax.sharding import PartitionSpec as P

HQ = 32
KV_HEADS = 4
N_DP = 4
GROUP = HQ // KV_HEADS
HEAD = 128
SPAN = 4
BLOCKS = SPAN + 1
QCOLS = GROUP * HEAD
KVCOLS = 2 * HEAD
COLS = QCOLS + BLOCKS * KVCOLS
FSTEP = 512
BSTEP = 400
CHUNKS = ((0, 2), (2, 2))
SCALE = 1.0 / math.sqrt(HEAD)
LOG2E = math.log2(math.e)
MASKED = -1e30
VMEM_LIMIT = 60 * 1024 * 1024
ATTEND_LIMIT = 32 * 1024 * 1024
SMALL_LIMIT = 8 * 1024 * 1024


def dot(a, b):
    return jnp.dot(a, b, preferred_element_type=jnp.float32)


def shifted(block, distance):
    devices = range(lax.axis_size("ctx"))
    route = [(i - distance, i) for i in devices if i - distance in devices]
    return lax.ppermute(block, "ctx", route)


def pack_kernel(order_ref, q_ref, k_ref, v_ref, *rest):
    out_ref = rest[-1]
    tok = q_ref.shape[0]
    n, grain, _ = out_ref.shape
    order = jnp.broadcast_to(order_ref[...].astype(jnp.float32), (tok, tok)).T
    column = lax.broadcasted_iota(jnp.int32, (tok, tok), 1)
    onehot = (order.astype(jnp.int32) == column).astype(jnp.bfloat16)
    q = dot(onehot, q_ref[...]).astype(jnp.bfloat16)
    out_ref[:, :, :QCOLS] = q.reshape(n, grain, QCOLS)
    kv = jnp.concatenate([k_ref[...], v_ref[...]], axis=1)
    kv = dot(onehot, kv).astype(jnp.bfloat16).reshape(n, grain, KVCOLS)
    ctx = n // N_DP
    for t in range(BLOCKS):
        back = SPAN - t
        at = QCOLS + t * KVCOLS
        for p in range(N_DP):
            if back:
                none = jnp.zeros((back, grain, KVCOLS), jnp.bfloat16)
                out_ref[p * ctx : p * ctx + back, :, at : at + KVCOLS] = none
            out_ref[p * ctx + back : (p + 1) * ctx, :, at : at + KVCOLS] = kv[
                p * ctx : (p + 1) * ctx - back
            ]


def first_pack_kernel(order_ref, q_ref, k_ref, v_ref, doc_ref, place_ref, out_ref, doc_out, place_out):
    doc_out[...] = doc_ref[...]
    place_out[...] = place_ref[...]
    pack_kernel(order_ref, q_ref, k_ref, v_ref, out_ref)


def pack(order, queries, keys, values, first, count, later=()):
    tok = queries.shape[0]
    devices = lax.axis_size("dp") * lax.axis_size("ctx")
    grain = tok // devices
    whole = [pl.BlockSpec(a.shape, lambda h: (0, 0)) for a in later]
    out = pl.pallas_call(
        first_pack_kernel if later else pack_kernel,
        grid=(count,),
        in_specs=[
            pl.BlockSpec(order.shape, lambda h: (0, 0)),
            pl.BlockSpec((tok, QCOLS), lambda h: (0, first + h)),
            pl.BlockSpec((tok, HEAD), lambda h: (0, first + h)),
            pl.BlockSpec((tok, HEAD), lambda h: (0, first + h)),
        ]
        + whole,
        out_specs=[pl.BlockSpec((devices, grain, COLS), lambda h: (0, 0, h))] + whole,
        out_shape=[jax.ShapeDtypeStruct((devices, grain, count * COLS), jnp.bfloat16)]
        + [jax.ShapeDtypeStruct(a.shape, a.dtype) for a in later],
        compiler_params=pltpu.CompilerParams(vmem_limit_bytes=VMEM_LIMIT),
        name="pack",
    )(order, queries, keys, values, *later)
    return out if later else out[0]


def tiles(half, low, high, tok, step, cut=None):
    low = max(low, half * tok // 2)
    high = min(high, SPAN * tok + (half + 1) * tok // 2)
    for low, high in ((low, high),) if cut is None else ((low, cut), (cut, high)):
        size = (high - low) // pl.cdiv(high - low, step)
        for i in range(low, high, size):
            yield slice(i, i + size)


def moved(here, base):
    return slice(here.start - base, here.stop - base)


def together(*work):
    work = list(work)
    while work:
        work = [w for w in work if next(w, work) is None]


def halves(unit, tok):
    half, pair = unit % 2, unit // 2
    rows = slice(half * tok // 2, (half + 1) * tok // 2)
    one, two = ((2 * pair + i) * HEAD for i in range(2))
    return half, rows, slice(one, one + HEAD), slice(two, two + HEAD)


def backward(half, low, high, p_of, ds_buf, q, do_s, dot_s, delta, k_all, v_all, kt, dk, dv, base, done):
    tok = q.shape[0]
    spans = list(tiles(half, low, high, tok, BSTEP))
    for here in spans:
        p = p_of(here)
        dp = dot(v_all[moved(here, base), :], dot_s[...])
        ds = (p.astype(jnp.float32) * (dp - delta[...])).astype(jnp.bfloat16)
        ds_buf[moved(here, spans[0].start), :] = ds
        yield
        dv[moved(here, base), :] += dot(p, do_s[...])
        dk[moved(here, base), :] += dot(ds, q[...])
        yield
    first, last = spans[0].start, spans[-1].stop
    done(dot(kt[:, first - base : last - base], ds_buf[: last - first, :]))
    yield


def store_heads(ref, value, rows, one, two):
    half = value.shape[0] // 2
    ref[rows, one] = value[:half]
    ref[rows, two] = value[half:]


def attend_body(
    cut, start_ref, place_ref, rx_ref, do_ref, att_ref, bias, k_all, v_all, kt, vt,
    q_loc, s_buf, ds_buf, dk, dv, p_of, saved, done, stop,
):
    tok = q_loc.shape[0]
    window = BLOCKS * tok
    reach = SPAN * tok + tok // 2

    @pl.when(pl.program_id(0) == 0)
    def _():
        u = lax.broadcasted_iota(jnp.int32, (reach, tok // 2), 0)
        t = lax.broadcasted_iota(jnp.int32, (reach, tok // 2), 1)
        for half in range(2):
            off = half * tok // 2
            start = start_ref[:, off : off + tok // 2] - off
            keep = (u >= start) & (u <= t + SPAN * tok)
            add = jnp.where(keep, 0.0, MASKED)
            bias[half, :, : tok // 2] = add
            bias[half, :, tok // 2 :] = add

    row = lax.broadcasted_iota(jnp.int32, (tok, tok), 0)
    rx = rx_ref[...].reshape(tok, COLS)
    for t in range(BLOCKS):
        spread = (place_ref[t : t + 1, :] == row).astype(jnp.bfloat16)
        at = QCOLS + t * KVCOLS
        kv = dot(spread, rx[:, at : at + KVCOLS])
        here = slice(t * tok, (t + 1) * tok)
        k_all[here, :] = kv[:, :HEAD].astype(jnp.bfloat16)
        v_all[here, :] = kv[:, HEAD:].astype(jnp.bfloat16)
        kt[:, here] = kv[:, :HEAD].T.astype(jnp.bfloat16)
        vt[:, here] = kv[:, HEAD:].T.astype(jnp.bfloat16)
        if t == SPAN:
            q_loc[...] = dot(spread, rx[:, :QCOLS]).astype(jnp.bfloat16)
    dk[...] = jnp.zeros_like(dk)
    dv[...] = jnp.zeros_like(dv)

    def forward(unit):
        half, rows, one, two = halves(unit, tok)
        off = half * tok // 2
        q_u, do_s, dot_s, delta = saved(unit)
        q = jnp.concatenate([q_loc[rows, one], q_loc[rows, two]], axis=0)
        q_u[...] = q
        qt = q.T
        top = jnp.full((1, tok), MASKED, jnp.float32)
        for here in tiles(half, 0, window, tok, FSTEP, cut):
            s = dot(k_all[here, :], qt) * (SCALE * LOG2E) + bias[half, moved(here, off), :]
            s_buf[moved(here, off), :] = s
            top = jnp.maximum(top, jnp.max(s, axis=0, keepdims=True))
            yield
        total = jnp.zeros((1, tok), jnp.float32)
        acc = None
        for here in tiles(half, 0, window, tok, FSTEP, cut):
            p = jnp.exp2(s_buf[moved(here, off), :] - top)
            total = total + jnp.sum(p, axis=0, keepdims=True)
            low = p.astype(jnp.bfloat16)
            p_of(unit, here)[...] = low
            part = dot(vt[:, here], low)
            acc = part if acc is None else acc + part
            yield
        inv = 1.0 / total
        att = (acc * inv).astype(jnp.bfloat16)
        store_heads(att_ref, att.T, rows, one, two)
        do = jnp.concatenate([do_ref[rows, one], do_ref[rows, two]], axis=0)
        scaled = (do.T.astype(jnp.float32) * inv).astype(jnp.bfloat16)
        dot_s[...] = scaled
        do_s[...] = scaled.T
        delta[...] = jnp.sum(
            scaled.astype(jnp.float32) * att.astype(jnp.float32), axis=0, keepdims=True
        )
        yield

    def back(unit):
        return backward(
            unit % 2, 0, stop, lambda here: p_of(unit, here)[...], ds_buf, *saved(unit),
            k_all, v_all, kt, dk, dv, 0, lambda dq: done(unit, dq),
        )

    together(forward(0))
    for unit in range(1, GROUP):
        together(forward(unit), back(unit - 1))
    together(back(GROUP - 1))


def store_terms(terms, dk, dv, tok, base=0):
    for t, term in enumerate(terms):
        here = slice(t * tok - base, (t + 1) * tok - base)
        term[:, :HEAD] = (dk[here, :] * SCALE).astype(term.dtype)
        term[:, HEAD:] = dv[here, :].astype(term.dtype)


def attend_kernel(*refs):
    start_ref, place_ref, rx_ref, do_ref, att_ref, dq_ref, far, near2, near1, own = refs[:10]
    bias, k_all, v_all, kt, vt, q_loc, s_buf, ds_buf, dk, dv = refs[10:20]
    slots = (refs[20:25], refs[25:30])
    tok = q_loc.shape[0]

    def p_of(unit, here):
        p_buf = slots[unit % 2][0]
        return p_buf.at[moved(here, unit % 2 * tok // 2), :]

    def saved(unit):
        return slots[unit % 2][1:]

    def done(unit, dq):
        _, rows, one, two = halves(unit, tok)
        store_heads(dq_ref, (dq * SCALE).T.astype(jnp.bfloat16), rows, one, two)

    attend_body(
        None, start_ref, place_ref, rx_ref, do_ref, att_ref, bias, k_all, v_all, kt, vt,
        q_loc, s_buf, ds_buf, dk, dv, p_of, saved, done, BLOCKS * tok,
    )
    store_terms((far.at[0], far.at[1], near2, near1, own), dk, dv, tok)


def scratch(tok):
    window, reach = BLOCKS * tok, SPAN * tok + tok // 2
    bf16, f32 = jnp.bfloat16, jnp.float32
    return [
        pltpu.VMEM((2, reach, tok), f32),
        pltpu.VMEM((window, HEAD), bf16),
        pltpu.VMEM((window, HEAD), bf16),
        pltpu.VMEM((HEAD, window), bf16),
        pltpu.VMEM((HEAD, window), bf16),
        pltpu.VMEM((tok, QCOLS), bf16),
        pltpu.VMEM((reach, tok), f32),
        pltpu.VMEM((reach, tok), bf16),
        pltpu.VMEM((window, HEAD), f32),
        pltpu.VMEM((window, HEAD), f32),
    ]


def kept(tok):
    bf16 = jnp.bfloat16
    return [
        ((tok, HEAD), bf16),
        ((tok, HEAD), bf16),
        ((HEAD, tok), bf16),
        ((1, tok), jnp.float32),
    ]


def estimate(count, share, tok):
    work = count * GROUP * BLOCKS * tok * tok
    return pl.CostEstimate(
        flops=int(share * 48 * work * HEAD),
        bytes_accessed=count * 4 * 1024 * 1024,
        transcendentals=work,
    )


def attend(start, places, rx, do, first, count, at=0):
    tok = do.shape[0]
    bf16, f32 = jnp.bfloat16, jnp.float32
    wide = pl.BlockSpec((tok, QCOLS), lambda h: (0, first + h))
    cols = pl.BlockSpec((tok, KVCOLS), lambda h: (0, h))
    slot = [pltpu.VMEM((SPAN * tok + tok // 2, tok), bf16)]
    slot += [pltpu.VMEM(*a) for a in kept(tok)]
    return pl.pallas_call(
        attend_kernel,
        grid=(count,),
        in_specs=[
            pl.BlockSpec(start.shape, lambda h: (0, 0)),
            pl.BlockSpec(places.shape, lambda h: (0, 0)),
            pl.BlockSpec((*rx.shape[:2], COLS), lambda h: (0, 0, at + h)),
            wide,
        ],
        out_specs=[wide, wide, pl.BlockSpec((2, tok, KVCOLS), lambda h: (0, 0, h)), cols, cols, cols],
        out_shape=[
            jax.ShapeDtypeStruct((tok, HQ * HEAD), bf16),
            jax.ShapeDtypeStruct((tok, HQ * HEAD), bf16),
            jax.ShapeDtypeStruct((2, tok, count * KVCOLS), bf16),
            jax.ShapeDtypeStruct((tok, count * KVCOLS), bf16),
            jax.ShapeDtypeStruct((tok, count * KVCOLS), bf16),
            jax.ShapeDtypeStruct((tok, count * KVCOLS), f32),
        ],
        scratch_shapes=scratch(tok) + slot + slot,
        compiler_params=pltpu.CompilerParams(vmem_limit_bytes=ATTEND_LIMIT),
        cost_estimate=estimate(count, 1.0, tok),
        name="attend",
    )(start, places, rx, do)


def attend_far_kernel(*refs):
    start_ref, place_ref, rx_ref, do_ref = refs[:4]
    att_ref, far, p_out, q_out, do_out, dot_out, delta_out, dq_out = refs[-23:-15]
    k_out, v_out, kt_out = refs[-15:-12]
    bias, k_all, v_all, kt, vt, q_loc, s_buf, ds_buf, dk, dv = refs[-12:-2]
    p_bufs = refs[-2:]
    tok = q_loc.shape[0]
    split = 2 * tok

    def p_of(unit, here):
        if here.start >= split:
            return p_out.at[unit, moved(here, split), :]
        return p_bufs[unit % 2].at[moved(here, unit % 2 * tok // 2), :]

    def saved(unit):
        return q_out.at[unit], do_out.at[unit], dot_out.at[unit], delta_out.at[unit]

    def done(unit, dq):
        dq_out[unit, :, :] = dq

    attend_body(
        split, start_ref, place_ref, rx_ref, do_ref, att_ref, bias, k_all, v_all, kt, vt,
        q_loc, s_buf, ds_buf, dk, dv, p_of, saved, done, split,
    )
    k_out[...] = k_all[split:, :]
    v_out[...] = v_all[split:, :]
    kt_out[...] = kt[:, split:]
    store_terms((far.at[0], far.at[1]), dk, dv, tok)


def attend_far(start, places, rx, do, old, first, at, after=()):
    tok = do.shape[0]
    count = rx.shape[2] // COLS
    near = BLOCKS * tok - 2 * tok
    bf16, f32 = jnp.bfloat16, jnp.float32
    wide = pl.BlockSpec((tok, QCOLS), lambda h: (0, first + at))
    state = [((near, tok), bf16)] + kept(tok) + [((HEAD, tok), f32)]
    state = [((GROUP, *shape), dtype) for shape, dtype in state]
    state += [((near, HEAD), bf16), ((near, HEAD), bf16), ((HEAD, near), bf16)]
    out = pl.pallas_call(
        attend_far_kernel,
        grid=(1,),
        in_specs=[
            pl.BlockSpec(start.shape, lambda h: (0, 0)),
            pl.BlockSpec(places.shape, lambda h: (0, 0)),
            pl.BlockSpec((*rx.shape[:2], COLS), lambda h: (0, 0, at)),
            wide,
        ]
        + [pl.BlockSpec(memory_space=pl.ANY)] * (len(old) + len(after)),
        out_specs=[wide, pl.BlockSpec((2, tok, KVCOLS), lambda h: (0, 0, at))]
        + [per_head(shape, at) for shape, _ in state],
        out_shape=[
            jax.ShapeDtypeStruct((tok, HQ * HEAD), bf16),
            jax.ShapeDtypeStruct((2, tok, count * KVCOLS), bf16),
        ]
        + [jax.ShapeDtypeStruct((count, *shape), dtype) for shape, dtype in state],
        scratch_shapes=scratch(tok) + [pltpu.VMEM((SPAN * tok + tok // 2, tok), bf16)] * 2,
        input_output_aliases={4 + i: i for i in range(len(old))},
        compiler_params=pltpu.CompilerParams(vmem_limit_bytes=ATTEND_LIMIT),
        cost_estimate=estimate(1, 0.6, tok),
        name="attend_far",
    )(start, places, rx, do, *old, *after)
    return out


def per_head(shape, at=None):
    zeros = [0] * len(shape)
    return pl.BlockSpec((None, *shape), lambda h: (h if at is None else at, *zeros))


def attend_near_kernel(*refs):
    p_in, q_in, do_in, dot_in, delta_in, dq_in, k_in, v_in, kt_in = refs[:9]
    dq_ref, near2, near1, own, dk, dv = refs[-8:-2]
    ds_bufs = refs[-2:]
    tok = near2.shape[0]
    split = 2 * tok
    dk[...] = jnp.zeros_like(dk)
    dv[...] = jnp.zeros_like(dv)

    def back(unit):
        def done(dq):
            _, rows, one, two = halves(unit, tok)
            dq = ((dq + dq_in[unit]) * SCALE).T.astype(jnp.bfloat16)
            store_heads(dq_ref, dq, rows, one, two)

        return backward(
            unit % 2, split, BLOCKS * tok, lambda here: p_in[unit, moved(here, split), :],
            ds_bufs[unit % 2], q_in.at[unit], do_in.at[unit], dot_in.at[unit],
            delta_in.at[unit], k_in, v_in, kt_in, dk, dv, split, done,
        )

    for unit in range(0, GROUP, 2):
        together(back(unit), back(unit + 1))
    store_terms((near2, near1, own), dk, dv, tok)


def attend_near(state, dq, first, count, after):
    tok = dq.shape[0]
    near = BLOCKS * tok - 2 * tok
    bf16, f32 = jnp.bfloat16, jnp.float32
    wide = pl.BlockSpec((tok, QCOLS), lambda h: (0, first + h))
    cols = pl.BlockSpec((tok, KVCOLS), lambda h: (0, h))
    return pl.pallas_call(
        attend_near_kernel,
        grid=(count,),
        in_specs=[per_head(a.shape[1:]) for a in state]
        + [pl.BlockSpec(memory_space=pl.ANY)] * (1 + len(after)),
        out_specs=[wide, cols, cols, cols],
        out_shape=[
            jax.ShapeDtypeStruct((tok, HQ * HEAD), bf16),
            jax.ShapeDtypeStruct((tok, count * KVCOLS), bf16),
            jax.ShapeDtypeStruct((tok, count * KVCOLS), bf16),
            jax.ShapeDtypeStruct((tok, count * KVCOLS), f32),
        ],
        scratch_shapes=[pltpu.VMEM((near, HEAD), f32)] * 2 + [pltpu.VMEM((near, tok), bf16)] * 2,
        input_output_aliases={len(state): 0},
        compiler_params=pltpu.CompilerParams(vmem_limit_bytes=ATTEND_LIMIT),
        cost_estimate=estimate(count, 0.4, tok),
        name="attend_near",
    )(*state, dq, *after)


def added(near, far):
    return (near[...].astype(jnp.float32) + far.astype(jnp.float32)).astype(jnp.bfloat16)


def merge_kernel(near2, near1, far, out2, out1):
    out2[...] = added(near2, far[0])
    out1[...] = added(near1, far[1])


def last_merge_kernel(near2, near1, far, own, back2, back1, out2, out1, total):
    merge_kernel(near2, near1, far, out2, out1)
    total[...] = own[...] + back2[...].astype(jnp.float32) + back1[...].astype(jnp.float32)


def merge(near2, near1, far, *own):
    shape = jax.ShapeDtypeStruct(near2.shape, jnp.bfloat16)
    total = [jax.ShapeDtypeStruct(a.shape, a.dtype) for a in own[:1]]
    return pl.pallas_call(
        last_merge_kernel if own else merge_kernel,
        out_shape=[shape, shape] + total,
        compiler_params=pltpu.CompilerParams(vmem_limit_bytes=SMALL_LIMIT),
        name="merge",
    )(near2, near1, far, *own)


def finish_kernel(done, own, back2, back1, gk_ref, gv_ref):
    width = own.shape[1]
    last = own[...] + back2[...].astype(jnp.float32) + back1[...].astype(jnp.float32)
    for at, total in ((0, done[...]), (width, last)):
        for i in range(width // KVCOLS):
            cols = slice((at // KVCOLS + i) * HEAD, (at // KVCOLS + i + 1) * HEAD)
            mid = i * KVCOLS + HEAD
            gk_ref[:, cols] = total[:, mid - HEAD : mid].astype(jnp.bfloat16)
            gv_ref[:, cols] = total[:, mid : mid + HEAD].astype(jnp.bfloat16)


def finish(*parts):
    tok = parts[0].shape[0]
    return pl.pallas_call(
        finish_kernel,
        out_shape=[jax.ShapeDtypeStruct((tok, KV_HEADS * HEAD), jnp.bfloat16)] * 2,
        compiler_params=pltpu.CompilerParams(vmem_limit_bytes=SMALL_LIMIT),
        name="finish",
    )(*parts)


def body(queries, keys, values, d_out, doc_ids, send_order, place):
    tok = queries.shape[0]
    shard = lax.axis_index("ctx")
    sent = []
    for first, count in CHUNKS:
        if first == 0:
            later = (doc_ids, place)
            packed, doc_ids, place = pack(send_order, queries, keys, values, first, count, later)
        else:
            packed = pack(send_order, queries, keys, values, first, count)
        sent.append(lax.all_to_all(packed, ("dp", "ctx"), split_axis=0, concat_axis=0, tiled=True))

    places = jnp.concatenate([shifted(place, SPAN - t) for t in range(SPAN)] + [place], axis=0)
    docs = jnp.pad(doc_ids[0], (SPAN * tok, 0), constant_values=-1)
    docs = lax.dynamic_slice_in_dim(docs, shard * tok, BLOCKS * tok, 0)
    before = docs[:, None] < docs[None, SPAN * tok :]
    start = jnp.sum(before.astype(jnp.int32), axis=0)[None, :]

    do = d_out[0]
    (first_a, count_a), (first_b, count_b) = CHUNKS
    att, dq, far_a, near2_a, near1_a, own_a = attend(start, places, sent[0], do, first_a, count_a)
    far_a = shifted(far_a, -2)
    half = attend_far(start, places, sent[1], do, (att,), first_b, 0)
    back2_a, back1_a = merge(near2_a, near1_a, far_a)
    after = (back1_a,)
    back2_a, back1_a = shifted(back2_a, -2), shifted(back1_a, -1)
    att, far_b, *state = attend_far(start, places, sent[1], do, half, first_b, 1, after)
    far_b = shifted(far_b, -2)
    dq, near2_b, near1_b, own_b = attend_near(state, dq, first_b, count_b, (back2_a, back1_a))
    back2_b, back1_b, total_a = merge(near2_b, near1_b, far_b, own_a, back2_a, back1_a)
    back2_b, back1_b = shifted(back2_b, -2), shifted(back1_b, -1)
    grad_k, grad_v = finish(total_a, own_b, back2_b, back1_b)
    return att[None], dq[None], grad_k[None], grad_v[None]


def solution(mesh):
    in_specs = (
        P(("dp", "ctx"), None),
        P(("dp", "ctx"), None),
        P(("dp", "ctx"), None),
        P("dp", "ctx", None),
        P("dp", None),
        P(("dp", "ctx"), None),
        P(("dp", "ctx"), None),
    )
    out_specs = (P("dp", "ctx", None),) * 4
    return jax.shard_map(body, mesh=mesh, in_specs=in_specs, out_specs=out_specs, check_vma=False)
```

profile of v0, /device:TPU:28, one launch (start us, length us, event | category | flops | bytes accessed | tf_op | source)
XLA Modules:
  0.0 143.4 jit_solution(13425613481521700568)
XLA Ops:
  0.6 3.3 %pack.2 = (bf16[128,2,4608]{2,1,0:T(2,128)(2,1)}, s32[1,8192]{1,0:T(1,128)}, s32[1,256]{1,0:T(1,128)}) custom-call(s32[1,256]{1,0:T(1,128)} %order_ref.3, bf16[256,4096]{1,0:T(8,128)(2,1)} %q_ref.3, bf16[256,512]{1,0:T(8,128)(2,1)} %k_ref.3, bf16[256,512]{1,0:T(8,128)(2,1)} %v_ref.3, s32[1,8192]{1,0:T(1,128)} %doc_ref.1, s32[1,256]{1,0:T(1,128)} %place_ref.1), custom_call_target="tpu_custom_call" | custom-call | tf_op jit(solution)/shard_map/pack/pallas_call | solution.py:77
  4.0 10.3 %all-to-all-start.1 = ((bf16[128,2,4608]{2,1,0:T(2,128)(2,1)}), bf16[128,2,4608]{2,1,0:T(2,128)(2,1)S(1)}, u32[]{:S(2)}, u32[]{:S(2)}) async-start(bf16[128,2,4608]{2,1,0:T(2,128)(2,1)} %get-tuple-element.48), calls=%async_computation.1 | async-start | bytes 4718592 | tf_op jit(solution)/shard_map/all_to_all | solution.py:505
  14.2 4.4 %collective-permute-start = (s32[1,256]{1,0:T(1,128)S(1)}, s32[1,256]{1,0:T(1,128)S(1)}, u32[]{:S(2)}, u32[]{:S(2)}) collective-permute-start(s32[1,256]{1,0:T(1,128)S(1)} %copy-done.3), channel_id=1, source_target_pairs={{0,4},{1,5},{2,6},{3,7},{4,8},{5,9},{6,10},{7,11},{8,12},{9,13},{1... | collective-permute-start | bytes 3080 | tf_op jit(solution)/shard_map/ppermute | solution.py:39
  18.7 4.1 %collective-permute-start.1 = (s32[1,256]{1,0:T(1,128)S(1)}, s32[1,256]{1,0:T(1,128)S(1)}, u32[]{:S(2)}, u32[]{:S(2)}) collective-permute-start(s32[1,256]{1,0:T(1,128)S(1)} %copy-done.3), channel_id=1, source_target_pairs={{0,3},{1,4},{2,5},{3,6},{4,7},{5,8},{6,9},{7,10},{8,11},{9,12},{10... | collective-permute-start | bytes 3080 | tf_op jit(solution)/shard_map/ppermute | solution.py:39
  22.7 3.4 %collective-permute-start.2 = (s32[1,256]{1,0:T(1,128)S(1)}, s32[1,256]{1,0:T(1,128)S(1)}, u32[]{:S(2)}, u32[]{:S(2)}) collective-permute-start(s32[1,256]{1,0:T(1,128)S(1)} %copy-done.3), channel_id=1, source_target_pairs={{0,2},{1,3},{2,4},{3,5},{4,6},{5,7},{6,8},{7,9},{8,10},{9,11},{10,... | collective-permute-start | bytes 3080 | tf_op jit(solution)/shard_map/ppermute | solution.py:39
  26.2 4.3 %collective-permute-start.3 = (s32[1,256]{1,0:T(1,128)S(1)}, s32[1,256]{1,0:T(1,128)S(1)}, u32[]{:S(2)}, u32[]{:S(2)}) collective-permute-start(s32[1,256]{1,0:T(1,128)S(1)} %copy-done.3), channel_id=1, source_target_pairs={{0,1},{1,2},{2,3},{3,4},{4,5},{5,6},{6,7},{7,8},{8,9},{9,10},{10,1... | collective-permute-start | bytes 3080 | tf_op jit(solution)/shard_map/ppermute | solution.py:39
  30.5 0.1 pad_dynamic-slice_fusion
  30.6 0.1 pad_dynamic-slice_fusion.1
  30.7 0.2 convert_reduce_fusion
  30.9 3.3 %pack.3 = bf16[128,2,4608]{2,1,0:T(2,128)(2,1)} custom-call(s32[1,256]{1,0:T(1,128)} %order_ref.3, bf16[256,4096]{1,0:T(8,128)(2,1)} %q_ref.3, bf16[256,512]{1,0:T(8,128)(2,1)} %k_ref.3, bf16[256,512]{1,0:T(8,128)(2,1)} %v_ref.3), custom_call_target="tpu_custom_call" | custom-call | tf_op jit(solution)/shard_map/pack/pallas_call | solution.py:77
  34.2 7.0 %collective-permute-done = s32[1,256]{1,0:T(1,128)S(1)} collective-permute-done((s32[1,256]{1,0:T(1,128)S(1)}, s32[1,256]{1,0:T(1,128)S(1)}, u32[]{:S(2)}, u32[]{:S(2)}) %collective-permute-start) | collective-permute-done | bytes 1056 | tf_op jit(solution)/shard_map/ppermute | solution.py:39
  41.2 3.0 %all-to-all-done.1.refs_2_ = bf16[128,2,4608]{2,1,0:T(2,128)(2,1)S(1)} async-done(((bf16[128,2,4608]{2,1,0:T(2,128)(2,1)}), bf16[128,2,4608]{2,1,0:T(2,128)(2,1)S(1)}, u32[]{:S(2)}, u32[]{:S(2)}) %all-to-all-start.1) | async-done | bytes 2359328 | tf_op jit(solution)/shard_map/all_to_all | solution.py:505
  44.2 8.5 %all-to-all-start = ((bf16[128,2,4608]{2,1,0:T(2,128)(2,1)}), bf16[128,2,4608]{2,1,0:T(2,128)(2,1)}, u32[]{:S(2)}, u32[]{:S(2)}) async-start(bf16[128,2,4608]{2,1,0:T(2,128)(2,1)} %pack.3), calls=%async_computation | async-start | bytes 4718592 | tf_op jit(solution)/shard_map/all_to_all | solution.py:505
  52.7 1.6 %copy-done = bf16[1,256,4096]{2,1,0:T(8,128)(2,1)S(1)} copy-done((bf16[1,256,4096]{2,1,0:T(8,128)(2,1)S(1)}, bf16[1,256,4096]{2,1,0:T(8,128)(2,1)}, u32[]{:S(2)}) %copy-start) | copy-done | bytes 2097176
  54.3 20.0 %attend.1 = (bf16[256,4096]{1,0:T(8,128)(2,1)}, bf16[256,4096]{1,0:T(8,128)(2,1)}, bf16[2,256,512]{2,1,0:T(8,128)(2,1)}, bf16[256,512]{1,0:T(8,128)(2,1)S(1)}, b...) custom-call(s32[1,256]{1,0:T(1,128)S(1)} %bitcast.7, s32[5,256]{1,0:T(8,128)S(1)} %concatenate.3.refs_1_, ...), custom_call_target="tpu_custom_call" | custom-call | flops 32212254720 | bytes 8388608 | tf_op jit(solution)/shard_map/attend/pallas_call | solution.py:302
  74.3 2.9 %collective-permute-start.4 = (bf16[2,256,512]{2,1,0:T(8,128)(2,1)}, bf16[2,256,512]{2,1,0:T(8,128)(2,1)S(1)}, u32[]{:S(2)}, u32[]{:S(2)}) collective-permute-start(bf16[2,256,512]{2,1,0:T(8,128)(2,1)} %get-tuple-element.63), channel_id=1, source_target_pairs={{2,0},{3,1},{4,2},{5,3},{6,4},{7,5},{8,6},{9,7},{10,8},{11,9},{12,... | collective-permute-start | bytes 1572872 | tf_op jit(solution)/shard_map/ppermute | solution.py:39
  77.2 5.1 %all-to-all-done.refs_2_ = bf16[128,2,4608]{2,1,0:T(2,128)(2,1)} async-done(((bf16[128,2,4608]{2,1,0:T(2,128)(2,1)}), bf16[128,2,4608]{2,1,0:T(2,128)(2,1)}, u32[]{:S(2)}, u32[]{:S(2)}) %all-to-all-start) | async-done | bytes 2359328 | tf_op jit(solution)/shard_map/all_to_all | solution.py:505
  82.3 1.6 %copy-done.1 = bf16[1,256,4096]{2,1,0:T(8,128)(2,1)S(1)} copy-done((bf16[1,256,4096]{2,1,0:T(8,128)(2,1)S(1)}, bf16[1,256,4096]{2,1,0:T(8,128)(2,1)}, u32[]{:S(2)}) %copy-start.1) | copy-done | bytes 2097176
  83.9 9.3 %attend_far.2 = (bf16[256,4096]{1,0:T(8,128)(2,1)}, bf16[2,256,512]{2,1,0:T(8,128)(2,1)S(1)}, bf16[2,8,768,256]{3,2,1,0:T(8,128)(2,1)S(1)}, bf16[2,8,256,128]{3,...) custom-call(s32[1,256]{1,0:T(1,128)S(1)} %bitcast.8, ...), custom_call_target="tpu_custom_call", output_to_operand_aliasing={{0}: (4, {})} | custom-call | flops 9663676416 | bytes 4194304 | tf_op jit(solution)/shard_map/attend_far/pallas_call | solution.py:366
  93.2 0.1 merge.2
  93.3 2.5 %collective-permute-start.5 = (bf16[256,512]{1,0:T(8,128)(2,1)S(1)}, bf16[256,512]{1,0:T(8,128)(2,1)S(1)}, u32[]{:S(2)}, u32[]{:S(2)}) collective-permute-start(bf16[256,512]{1,0:T(8,128)(2,1)S(1)} %get-tuple-element.76), channel_id=1, source_target_pairs={{2,0},{3,1},{4,2},{5,3},{6,4},{7,5},{8,6},{9,7},{10,8},{11,9},{12,... | collective-permute-start | bytes 786440 | tf_op jit(solution)/shard_map/ppermute | solution.py:39
  95.9 3.8 %collective-permute-start.6 = (bf16[256,512]{1,0:T(8,128)(2,1)S(1)}, bf16[256,512]{1,0:T(8,128)(2,1)S(1)}, u32[]{:S(2)}, u32[]{:S(2)}) collective-permute-start(bf16[256,512]{1,0:T(8,128)(2,1)S(1)} %get-tuple-element.64.refs_15_), channel_id=1, source_target_pairs={{1,0},{2,1},{3,2},{4,3},{5,4},{6,5},{7,6},{8,7},{9,8},{10,9},{11,1... | collective-permute-start | bytes 786440 | tf_op jit(solution)/shard_map/ppermute | solution.py:39
  99.7 9.3 %attend_far.3 = (bf16[256,4096]{1,0:T(8,128)(2,1)}, bf16[2,256,512]{2,1,0:T(8,128)(2,1)S(1)}, bf16[2,8,768,256]{3,2,1,0:T(8,128)(2,1)S(1)}, bf16[2,8,256,128]{3,...) custom-call(s32[1,256]{1,0:T(1,128)S(1)} %bitcast.9, ...), custom_call_target="tpu_custom_call", output_to_operand_aliasing={{0}: (4, {}), {1}: (5, {}), {2}: (6, {}), {3}: (7, {}), {4}... | custom-call | flops 9663676416 | bytes 4194304 | tf_op jit(solution)/shard_map/attend_far/pallas_call | solution.py:366
  109.0 3.5 %collective-permute-start.7 = (bf16[2,256,512]{2,1,0:T(8,128)(2,1)S(1)}, bf16[2,256,512]{2,1,0:T(8,128)(2,1)S(1)}, u32[]{:S(2)}, u32[]{:S(2)}) collective-permute-start(bf16[2,256,512]{2,1,0:T(8,128)(2,1)S(1)} %get-tuple-element.80), channel_id=1, source_target_pairs={{2,0},{3,1},{4,2},{5,3},{6,4},{7,5},{8,6},{9,7},{10,8},{11,9},{12,... | collective-permute-start | bytes 1572872 | tf_op jit(solution)/shard_map/ppermute | solution.py:39
  112.5 6.7 %attend_near.1 = (bf16[256,4096]{1,0:T(8,128)(2,1)}, bf16[256,512]{1,0:T(8,128)(2,1)S(1)}, bf16[256,512]{1,0:T(8,128)(2,1)S(1)}, f32[256,512]{1,0:T(8,128)S(1)}) custom-call(bf16[2,8,768,256]{3,2,1,0:T(8,128)(2,1)S(1)} %get-tuple-element.66.refs_0_, bf16[2,8,256,128]{3,2,1,0:T(8,128)(2,1)S(1)} %get-tuple-element.67.refs_1_, ...), custom_call_target="tpu_custom_call", output_to_operand_aliasing={{0}: (9, {})} | custom-call | flops 12884901888 | bytes 8388608 | tf_op jit(solution)/shard_map/attend_near/pallas_call | solution.py:429
  119.2 6.9 %collective-permute-done.7.far = bf16[2,256,512]{2,1,0:T(8,128)(2,1)S(1)} collective-permute-done((bf16[2,256,512]{2,1,0:T(8,128)(2,1)S(1)}, bf16[2,256,512]{2,1,0:T(8,128)(2,1)S(1)}, u32[]{:S(2)}, u32[]{:S(2)}) %collective-permute-start.7) | collective-permute-done | bytes 524320 | tf_op jit(solution)/shard_map/ppermute | solution.py:39
  126.1 0.2 merge.3
  126.3 2.3 %collective-permute-start.8 = (bf16[256,512]{1,0:T(8,128)(2,1)S(1)}, bf16[256,512]{1,0:T(8,128)(2,1)S(1)}, u32[]{:S(2)}, u32[]{:S(2)}) collective-permute-start(bf16[256,512]{1,0:T(8,128)(2,1)S(1)} %get-tuple-element.84), channel_id=1, source_target_pairs={{2,0},{3,1},{4,2},{5,3},{6,4},{7,5},{8,6},{9,7},{10,8},{11,9},{12,... | collective-permute-start | bytes 786440 | tf_op jit(solution)/shard_map/ppermute | solution.py:39
  128.6 4.3 %collective-permute-start.9 = (bf16[256,512]{1,0:T(8,128)(2,1)S(1)}, bf16[256,512]{1,0:T(8,128)(2,1)S(1)}, u32[]{:S(2)}, u32[]{:S(2)}) collective-permute-start(bf16[256,512]{1,0:T(8,128)(2,1)S(1)} %get-tuple-element.85), channel_id=1, source_target_pairs={{1,0},{2,1},{3,2},{4,3},{5,4},{6,5},{7,6},{8,7},{9,8},{10,9},{11,1... | collective-permute-start | bytes 786440 | tf_op jit(solution)/shard_map/ppermute | solution.py:39
  133.0 6.4 %collective-permute-done.8.back2 = bf16[256,512]{1,0:T(8,128)(2,1)S(1)} collective-permute-done((bf16[256,512]{1,0:T(8,128)(2,1)S(1)}, bf16[256,512]{1,0:T(8,128)(2,1)S(1)}, u32[]{:S(2)}, u32[]{:S(2)}) %collective-permute-start.8) | collective-permute-done | bytes 262176 | tf_op jit(solution)/shard_map/ppermute | solution.py:39
  139.4 3.1 %collective-permute-done.9.back1 = bf16[256,512]{1,0:T(8,128)(2,1)S(1)} collective-permute-done((bf16[256,512]{1,0:T(8,128)(2,1)S(1)}, bf16[256,512]{1,0:T(8,128)(2,1)S(1)}, u32[]{:S(2)}, u32[]{:S(2)}) %collective-permute-start.9) | collective-permute-done | bytes 262176 | tf_op jit(solution)/shard_map/ppermute | solution.py:39
  142.5 0.9 finish.1
  (13 shorter events, 0.1 us)
Async XLA Ops:
  4.0 10.3 %copy-start.3 = (s32[1,256]{1,0:T(1,128)S(1)}, s32[1,256]{1,0:T(1,128)}, u32[]{:S(2)}) copy-start(s32[1,256]{1,0:T(1,128)} %get-tuple-element.47) | copy-start | bytes 3076
  4.0 26.5 %copy-start.2 = (s32[1,8192]{1,0:T(1,128)S(1)}, s32[1,8192]{1,0:T(1,128)}, u32[]{:S(2)}) copy-start(s32[1,8192]{1,0:T(1,128)} %get-tuple-element.46) | copy-start | bytes 98308
  4.0 40.2 %all-to-all-start.1 = ((bf16[128,2,4608]{2,1,0:T(2,128)(2,1)}), bf16[128,2,4608]{2,1,0:T(2,128)(2,1)S(1)}, u32[]{:S(2)}, u32[]{:S(2)}) async-start(bf16[128,2,4608]{2,1,0:T(2,128)(2,1)} %get-tuple-element.48), calls=%async_computation.1 | async-start | bytes 4718592 | tf_op jit(solution)/shard_map/all_to_all | solution.py:505
  14.2 27.0 %collective-permute-start = (s32[1,256]{1,0:T(1,128)S(1)}, s32[1,256]{1,0:T(1,128)S(1)}, u32[]{:S(2)}, u32[]{:S(2)}) collective-permute-start(s32[1,256]{1,0:T(1,128)S(1)} %copy-done.3), channel_id=1, source_target_pairs={{0,4},{1,5},{2,6},{3,7},{4,8},{5,9},{6,10},{7,11},{8,12},{9,13},{1... | collective-permute-start | bytes 3080 | tf_op jit(solution)/shard_map/ppermute | solution.py:39
  18.7 22.5 %collective-permute-start.1 = (s32[1,256]{1,0:T(1,128)S(1)}, s32[1,256]{1,0:T(1,128)S(1)}, u32[]{:S(2)}, u32[]{:S(2)}) collective-permute-start(s32[1,256]{1,0:T(1,128)S(1)} %copy-done.3), channel_id=1, source_target_pairs={{0,3},{1,4},{2,5},{3,6},{4,7},{5,8},{6,9},{7,10},{8,11},{9,12},{10... | collective-permute-start | bytes 3080 | tf_op jit(solution)/shard_map/ppermute | solution.py:39
  22.7 18.5 %collective-permute-start.2 = (s32[1,256]{1,0:T(1,128)S(1)}, s32[1,256]{1,0:T(1,128)S(1)}, u32[]{:S(2)}, u32[]{:S(2)}) collective-permute-start(s32[1,256]{1,0:T(1,128)S(1)} %copy-done.3), channel_id=1, source_target_pairs={{0,2},{1,3},{2,4},{3,5},{4,6},{5,7},{6,8},{7,9},{8,10},{9,11},{10,... | collective-permute-start | bytes 3080 | tf_op jit(solution)/shard_map/ppermute | solution.py:39
  26.2 15.0 %collective-permute-start.3 = (s32[1,256]{1,0:T(1,128)S(1)}, s32[1,256]{1,0:T(1,128)S(1)}, u32[]{:S(2)}, u32[]{:S(2)}) collective-permute-start(s32[1,256]{1,0:T(1,128)S(1)} %copy-done.3), channel_id=1, source_target_pairs={{0,1},{1,2},{2,3},{3,4},{4,5},{5,6},{6,7},{7,8},{8,9},{9,10},{10,1... | collective-permute-start | bytes 3080 | tf_op jit(solution)/shard_map/ppermute | solution.py:39
  44.2 38.1 %all-to-all-start = ((bf16[128,2,4608]{2,1,0:T(2,128)(2,1)}), bf16[128,2,4608]{2,1,0:T(2,128)(2,1)}, u32[]{:S(2)}, u32[]{:S(2)}) async-start(bf16[128,2,4608]{2,1,0:T(2,128)(2,1)} %pack.3), calls=%async_computation | async-start | bytes 4718592 | tf_op jit(solution)/shard_map/all_to_all | solution.py:505
  52.7 1.6 %copy-start = (bf16[1,256,4096]{2,1,0:T(8,128)(2,1)S(1)}, bf16[1,256,4096]{2,1,0:T(8,128)(2,1)}, u32[]{:S(2)}) copy-start(bf16[1,256,4096]{2,1,0:T(8,128)(2,1)} %param.10) | copy-start | bytes 6291460
  74.3 18.9 %collective-permute-start.4 = (bf16[2,256,512]{2,1,0:T(8,128)(2,1)}, bf16[2,256,512]{2,1,0:T(8,128)(2,1)S(1)}, u32[]{:S(2)}, u32[]{:S(2)}) collective-permute-start(bf16[2,256,512]{2,1,0:T(8,128)(2,1)} %get-tuple-element.63), channel_id=1, source_target_pairs={{2,0},{3,1},{4,2},{5,3},{6,4},{7,5},{8,6},{9,7},{10,8},{11,9},{12,... | collective-permute-start | bytes 1572872 | tf_op jit(solution)/shard_map/ppermute | solution.py:39
  82.3 1.6 %copy-start.1 = (bf16[1,256,4096]{2,1,0:T(8,128)(2,1)S(1)}, bf16[1,256,4096]{2,1,0:T(8,128)(2,1)}, u32[]{:S(2)}) copy-start(bf16[1,256,4096]{2,1,0:T(8,128)(2,1)} %param.10) | copy-start | bytes 6291460
  93.3 19.1 %collective-permute-start.5 = (bf16[256,512]{1,0:T(8,128)(2,1)S(1)}, bf16[256,512]{1,0:T(8,128)(2,1)S(1)}, u32[]{:S(2)}, u32[]{:S(2)}) collective-permute-start(bf16[256,512]{1,0:T(8,128)(2,1)S(1)} %get-tuple-element.76), channel_id=1, source_target_pairs={{2,0},{3,1},{4,2},{5,3},{6,4},{7,5},{8,6},{9,7},{10,8},{11,9},{12,... | collective-permute-start | bytes 786440 | tf_op jit(solution)/shard_map/ppermute | solution.py:39
  95.9 16.6 %collective-permute-start.6 = (bf16[256,512]{1,0:T(8,128)(2,1)S(1)}, bf16[256,512]{1,0:T(8,128)(2,1)S(1)}, u32[]{:S(2)}, u32[]{:S(2)}) collective-permute-start(bf16[256,512]{1,0:T(8,128)(2,1)S(1)} %get-tuple-element.64.refs_15_), channel_id=1, source_target_pairs={{1,0},{2,1},{3,2},{4,3},{5,4},{6,5},{7,6},{8,7},{9,8},{10,9},{11,1... | collective-permute-start | bytes 786440 | tf_op jit(solution)/shard_map/ppermute | solution.py:39
  109.0 17.1 %collective-permute-start.7 = (bf16[2,256,512]{2,1,0:T(8,128)(2,1)S(1)}, bf16[2,256,512]{2,1,0:T(8,128)(2,1)S(1)}, u32[]{:S(2)}, u32[]{:S(2)}) collective-permute-start(bf16[2,256,512]{2,1,0:T(8,128)(2,1)S(1)} %get-tuple-element.80), channel_id=1, source_target_pairs={{2,0},{3,1},{4,2},{5,3},{6,4},{7,5},{8,6},{9,7},{10,8},{11,9},{12,... | collective-permute-start | bytes 1572872 | tf_op jit(solution)/shard_map/ppermute | solution.py:39
  126.3 13.1 %collective-permute-start.8 = (bf16[256,512]{1,0:T(8,128)(2,1)S(1)}, bf16[256,512]{1,0:T(8,128)(2,1)S(1)}, u32[]{:S(2)}, u32[]{:S(2)}) collective-permute-start(bf16[256,512]{1,0:T(8,128)(2,1)S(1)} %get-tuple-element.84), channel_id=1, source_target_pairs={{2,0},{3,1},{4,2},{5,3},{6,4},{7,5},{8,6},{9,7},{10,8},{11,9},{12,... | collective-permute-start | bytes 786440 | tf_op jit(solution)/shard_map/ppermute | solution.py:39
  128.6 13.8 %collective-permute-start.9 = (bf16[256,512]{1,0:T(8,128)(2,1)S(1)}, bf16[256,512]{1,0:T(8,128)(2,1)S(1)}, u32[]{:S(2)}, u32[]{:S(2)}) collective-permute-start(bf16[256,512]{1,0:T(8,128)(2,1)S(1)} %get-tuple-element.85), channel_id=1, source_target_pairs={{1,0},{2,1},{3,2},{4,3},{5,4},{6,5},{7,6},{8,7},{9,8},{10,9},{11,1... | collective-permute-start | bytes 786440 | tf_op jit(solution)/shard_map/ppermute | solution.py:39
where the time goes:
time: 145 us; the launch traced here: 143 us
  starting transfers between devices  54.4 us (38%)
  Pallas kernels  53.2 us (37%)
  waiting for transfers between devices  31.4 us (22%)
  local copies, waits for them, and re-layouts  3.37 us (2%)
    ppermute x10, starting transfers between devices, shifted(): return lax.ppermute(block, 'ctx', route)  35.6 us
    ppermute x10, waiting for transfers between devices, shifted(): return lax.ppermute(block, 'ctx', route)  23.3 us
    pallas_call x1, Pallas kernels, attend(): pl.pallas_call(attend_kernel, grid=(count,), in_specs=[pl.BlockSpec(start...  20 us
    all_to_all x2, starting transfers between devices, body(): lax.all_to_all(packed, ('dp', 'ctx'), split_axis=0, concat_axis=0, tiled=...  18.7 us
    pallas_call x2, Pallas kernels, attend_far(): pl.pallas_call(attend_far_kernel, grid=(1,), in_specs=[pl.BlockSpec(start...  18.6 us
    all_to_all x2, waiting for transfers between devices, body(): lax.all_to_all(packed, ('dp', 'ctx'), split_axis=0, concat_axis=0, tiled=...  8.04 us
    pallas_call x1, Pallas kernels, attend_near(): pl.pallas_call(attend_near_kernel, grid=(count,), in_specs=[per_head(a.sh...  6.68 us
    pallas_call x2, Pallas kernels, pack(): pl.pallas_call(first_pack_kernel if later else pack_kernel, grid=(count,)...  6.65 us
  transfers between devices with their start and end apart: 12, of which 6 were waited for; matrix products, arithmetic and copies ran while one was open for 0% of the time, Pallas kernels for 34%

commit v1 on v0

--- a/solution.py
+++ b/solution.py
@@ -19,13 +19,14 @@
 KVCOLS = 2 * HEAD
 COLS = QCOLS + BLOCKS * KVCOLS
 FSTEP = 512
-BSTEP = 400
+BSTEP = 600
 CHUNKS = ((0, 2), (2, 2))
 SCALE = 1.0 / math.sqrt(HEAD)
 LOG2E = math.log2(math.e)
 MASKED = -1e30
 VMEM_LIMIT = 60 * 1024 * 1024
 ATTEND_LIMIT = 32 * 1024 * 1024
+FAR_LIMIT = 32 * 1024 * 1024
 SMALL_LIMIT = 8 * 1024 * 1024
 
 
@@ -188,13 +189,13 @@
         top = jnp.full((1, tok), MASKED, jnp.float32)
         for here in tiles(half, 0, window, tok, FSTEP, cut):
             s = dot(k_all[here, :], qt) * (SCALE * LOG2E) + bias[half, moved(here, off), :]
-            s_buf[moved(here, off), :] = s
+            s_buf[unit % 2, moved(here, off), :] = s
             top = jnp.maximum(top, jnp.max(s, axis=0, keepdims=True))
             yield
         total = jnp.zeros((1, tok), jnp.float32)
         acc = None
         for here in tiles(half, 0, window, tok, FSTEP, cut):
-            p = jnp.exp2(s_buf[moved(here, off), :] - top)
+            p = jnp.exp2(s_buf[unit % 2, moved(here, off), :] - top)
             total = total + jnp.sum(p, axis=0, keepdims=True)
             low = p.astype(jnp.bfloat16)
             p_of(unit, here)[...] = low
@@ -215,14 +216,14 @@
 
     def back(unit):
         return backward(
-            unit % 2, 0, stop, lambda here: p_of(unit, here)[...], ds_buf, *saved(unit),
+            unit % 2, 0, stop, lambda here: p_of(unit, here)[...], ds_buf.at[unit % 2], *saved(unit),
             k_all, v_all, kt, dk, dv, 0, lambda dq: done(unit, dq),
         )
 
-    together(forward(0))
-    for unit in range(1, GROUP):
-        together(forward(unit), back(unit - 1))
-    together(back(GROUP - 1))
+    together(forward(0), forward(1))
+    for unit in range(2, GROUP, 2):
+        together(forward(unit), back(unit - 2), forward(unit + 1), back(unit - 1))
+    together(back(GROUP - 2), back(GROUP - 1))
 
 
 def store_terms(terms, dk, dv, tok, base=0):
@@ -235,19 +236,19 @@
 def attend_kernel(*refs):
     start_ref, place_ref, rx_ref, do_ref, att_ref, dq_ref, far, near2, near1, own = refs[:10]
     bias, k_all, v_all, kt, vt, q_loc, s_buf, ds_buf, dk, dv = refs[10:20]
-    slots = (refs[20:25], refs[25:30])
+    slots = [refs[20 + 5 * i : 25 + 5 * i] for i in range(4)]
     tok = q_loc.shape[0]
 
     def p_of(unit, here):
-        p_buf = slots[unit % 2][0]
+        p_buf = slots[unit % 4][0]
         return p_buf.at[moved(here, unit % 2 * tok // 2), :]
 
     def saved(unit):
-        return slots[unit % 2][1:]
+        return slots[unit % 4][1:]
 
     def done(unit, dq):
         _, rows, one, two = halves(unit, tok)
-        store_heads(dq_ref, (dq * SCALE).T.astype(jnp.bfloat16), rows, one, two)
+        store_heads(dq_ref, (dq * SCALE).astype(jnp.bfloat16).T, rows, one, two)
 
     attend_body(
         None, start_ref, place_ref, rx_ref, do_ref, att_ref, bias, k_all, v_all, kt, vt,
@@ -266,8 +267,8 @@
         pltpu.VMEM((HEAD, window), bf16),
         pltpu.VMEM((HEAD, window), bf16),
         pltpu.VMEM((tok, QCOLS), bf16),
-        pltpu.VMEM((reach, tok), f32),
-        pltpu.VMEM((reach, tok), bf16),
+        pltpu.VMEM((2, reach, tok), f32),
+        pltpu.VMEM((2, reach, tok), bf16),
         pltpu.VMEM((window, HEAD), f32),
         pltpu.VMEM((window, HEAD), f32),
     ]
@@ -306,7 +307,7 @@
             pl.BlockSpec(start.shape, lambda h: (0, 0)),
             pl.BlockSpec(places.shape, lambda h: (0, 0)),
             pl.BlockSpec((*rx.shape[:2], COLS), lambda h: (0, 0, at + h)),
-            wide,
+            pl.BlockSpec((tok, QCOLS), lambda h: (0, h)),
         ],
         out_specs=[wide, wide, pl.BlockSpec((2, tok, KVCOLS), lambda h: (0, 0, h)), cols, cols, cols],
         out_shape=[
@@ -317,7 +318,7 @@
             jax.ShapeDtypeStruct((tok, count * KVCOLS), bf16),
             jax.ShapeDtypeStruct((tok, count * KVCOLS), f32),
         ],
-        scratch_shapes=scratch(tok) + slot + slot,
+        scratch_shapes=scratch(tok) + slot * 4,
         compiler_params=pltpu.CompilerParams(vmem_limit_bytes=ATTEND_LIMIT),
         cost_estimate=estimate(count, 1.0, tok),
         name="attend",
@@ -326,17 +327,17 @@
 
 def attend_far_kernel(*refs):
     start_ref, place_ref, rx_ref, do_ref = refs[:4]
-    att_ref, far, p_out, q_out, do_out, dot_out, delta_out, dq_out = refs[-23:-15]
-    k_out, v_out, kt_out = refs[-15:-12]
-    bias, k_all, v_all, kt, vt, q_loc, s_buf, ds_buf, dk, dv = refs[-12:-2]
-    p_bufs = refs[-2:]
+    att_ref, far, p_out, q_out, do_out, dot_out, delta_out, dq_out = refs[-25:-17]
+    k_out, v_out, kt_out = refs[-17:-14]
+    bias, k_all, v_all, kt, vt, q_loc, s_buf, ds_buf, dk, dv = refs[-14:-4]
+    p_bufs = refs[-4:]
     tok = q_loc.shape[0]
     split = 2 * tok
 
     def p_of(unit, here):
         if here.start >= split:
             return p_out.at[unit, moved(here, split), :]
-        return p_bufs[unit % 2].at[moved(here, unit % 2 * tok // 2), :]
+        return p_bufs[unit % 4].at[moved(here, unit % 2 * tok // 2), :]
 
     def saved(unit):
         return q_out.at[unit], do_out.at[unit], dot_out.at[unit], delta_out.at[unit]
@@ -354,44 +355,43 @@
     store_terms((far.at[0], far.at[1]), dk, dv, tok)
 
 
-def attend_far(start, places, rx, do, old, first, at, after=()):
+def attend_far(start, places, rx, do, att, first):
     tok = do.shape[0]
     count = rx.shape[2] // COLS
     near = BLOCKS * tok - 2 * tok
     bf16, f32 = jnp.bfloat16, jnp.float32
-    wide = pl.BlockSpec((tok, QCOLS), lambda h: (0, first + at))
+    wide = pl.BlockSpec((tok, QCOLS), lambda h: (0, first + h))
     state = [((near, tok), bf16)] + kept(tok) + [((HEAD, tok), f32)]
     state = [((GROUP, *shape), dtype) for shape, dtype in state]
     state += [((near, HEAD), bf16), ((near, HEAD), bf16), ((HEAD, near), bf16)]
     out = pl.pallas_call(
         attend_far_kernel,
-        grid=(1,),
+        grid=(count,),
         in_specs=[
             pl.BlockSpec(start.shape, lambda h: (0, 0)),
             pl.BlockSpec(places.shape, lambda h: (0, 0)),
-            pl.BlockSpec((*rx.shape[:2], COLS), lambda h: (0, 0, at)),
-            wide,
-        ]
-        + [pl.BlockSpec(memory_space=pl.ANY)] * (len(old) + len(after)),
-        out_specs=[wide, pl.BlockSpec((2, tok, KVCOLS), lambda h: (0, 0, at))]
-        + [per_head(shape, at) for shape, _ in state],
+            pl.BlockSpec((*rx.shape[:2], COLS), lambda h: (0, 0, h)),
+            pl.BlockSpec((tok, QCOLS), lambda h: (0, h)),
+            pl.BlockSpec(memory_space=pl.ANY),
+        ],
+        out_specs=[wide, pl.BlockSpec((2, tok, KVCOLS), lambda h: (0, 0, h))]
+        + [per_head(shape) for shape, _ in state],
         out_shape=[
             jax.ShapeDtypeStruct((tok, HQ * HEAD), bf16),
             jax.ShapeDtypeStruct((2, tok, count * KVCOLS), bf16),
         ]
         + [jax.ShapeDtypeStruct((count, *shape), dtype) for shape, dtype in state],
-        scratch_shapes=scratch(tok) + [pltpu.VMEM((SPAN * tok + tok // 2, tok), bf16)] * 2,
-        input_output_aliases={4 + i: i for i in range(len(old))},
-        compiler_params=pltpu.CompilerParams(vmem_limit_bytes=ATTEND_LIMIT),
-        cost_estimate=estimate(1, 0.6, tok),
+        scratch_shapes=scratch(tok) + [pltpu.VMEM((SPAN * tok + tok // 2, tok), bf16)] * 4,
+        input_output_aliases={4: 0},
+        compiler_params=pltpu.CompilerParams(vmem_limit_bytes=FAR_LIMIT),
+        cost_estimate=estimate(count, 0.6, tok),
         name="attend_far",
-    )(start, places, rx, do, *old, *after)
+    )(start, places, rx, do, att)
     return out
 
 
-def per_head(shape, at=None):
-    zeros = [0] * len(shape)
-    return pl.BlockSpec((None, *shape), lambda h: (h if at is None else at, *zeros))
+def per_head(shape):
+    return pl.BlockSpec((None, *shape), lambda h: (h, *([0] * len(shape))))
 
 
 def attend_near_kernel(*refs):
@@ -406,7 +406,7 @@
     def back(unit):
         def done(dq):
             _, rows, one, two = halves(unit, tok)
-            dq = ((dq + dq_in[unit]) * SCALE).T.astype(jnp.bfloat16)
+            dq = ((dq + dq_in[unit]) * SCALE).astype(jnp.bfloat16).T
             store_heads(dq_ref, dq, rows, one, two)
 
         return backward(
@@ -446,36 +446,58 @@
     )(*state, dq, *after)
 
 
+def split_kernel(do_ref, _, *outs):
+    at = 0
+    for out in outs:
+        out[...] = do_ref[:, at : at + out.shape[1]]
+        at += out.shape[1]
+
+
+def split(do, after, counts):
+    tok = do.shape[0]
+    return pl.pallas_call(
+        split_kernel,
+        grid=(1,),
+        in_specs=[pl.BlockSpec(do.shape, lambda h: (0, 0)), pl.BlockSpec(memory_space=pl.ANY)],
+        out_specs=[pl.BlockSpec((tok, n * QCOLS), lambda h: (0, 0)) for n in counts],
+        out_shape=[jax.ShapeDtypeStruct((tok, n * QCOLS), jnp.bfloat16) for n in counts],
+        compiler_params=pltpu.CompilerParams(vmem_limit_bytes=VMEM_LIMIT),
+        name="split",
+    )(do, after)
+
+
 def added(near, far):
     return (near[...].astype(jnp.float32) + far.astype(jnp.float32)).astype(jnp.bfloat16)
 
 
-def merge_kernel(near2, near1, far, out2, out1):
+def near1_kernel(near1, far, *rest):
+    out1 = rest[-1]
+    out1[...] = added(near1, far[1])
+
+
+def near2_kernel(near2, far, out2):
     out2[...] = added(near2, far[0])
-    out1[...] = added(near1, far[1])
-
-
-def last_merge_kernel(near2, near1, far, own, back2, back1, out2, out1, total):
-    merge_kernel(near2, near1, far, out2, out1)
-    total[...] = own[...] + back2[...].astype(jnp.float32) + back1[...].astype(jnp.float32)
-
-
-def merge(near2, near1, far, *own):
-    shape = jax.ShapeDtypeStruct(near2.shape, jnp.bfloat16)
-    total = [jax.ShapeDtypeStruct(a.shape, a.dtype) for a in own[:1]]
+
+
+def last_near2_kernel(near2, far, _, out2):
+    out2[...] = added(near2, far[0])
+
+
+def merge(kernel, outs, *args):
     return pl.pallas_call(
-        last_merge_kernel if own else merge_kernel,
-        out_shape=[shape, shape] + total,
+        kernel,
+        out_shape=[jax.ShapeDtypeStruct(a.shape, a.dtype) for a in outs],
         compiler_params=pltpu.CompilerParams(vmem_limit_bytes=SMALL_LIMIT),
         name="merge",
-    )(near2, near1, far, *own)
-
-
-def finish_kernel(done, own, back2, back1, gk_ref, gv_ref):
-    width = own.shape[1]
-    last = own[...] + back2[...].astype(jnp.float32) + back1[...].astype(jnp.float32)
-    for at, total in ((0, done[...]), (width, last)):
-        for i in range(width // KVCOLS):
+    )(*args)
+
+
+def finish_kernel(own_a, back2_a, back1_a, own_b, back2_b, back1_b, gk_ref, gv_ref):
+    width = own_a.shape[1]
+    a, b = (own_a, back2_a, back1_a), (own_b, back2_b, back1_b)
+    for at, (own, back2, back1) in ((0, a), (width, b)):
+        total = own[...] + back2[...].astype(jnp.float32) + back1[...].astype(jnp.float32)
+        for i in range(own.shape[1] // KVCOLS):
             cols = slice((at // KVCOLS + i) * HEAD, (at // KVCOLS + i + 1) * HEAD)
             mid = i * KVCOLS + HEAD
             gk_ref[:, cols] = total[:, mid - HEAD : mid].astype(jnp.bfloat16)
@@ -510,20 +532,20 @@
     before = docs[:, None] < docs[None, SPAN * tok :]
     start = jnp.sum(before.astype(jnp.int32), axis=0)[None, :]
 
-    do = d_out[0]
     (first_a, count_a), (first_b, count_b) = CHUNKS
-    att, dq, far_a, near2_a, near1_a, own_a = attend(start, places, sent[0], do, first_a, count_a)
+    do_a, do_b = split(d_out[0], doc_ids, (count_a, count_b))
+    att, dq, far_a, near2_a, near1_a, own_a = attend(start, places, sent[0], do_a, first_a, count_a)
     far_a = shifted(far_a, -2)
-    half = attend_far(start, places, sent[1], do, (att,), first_b, 0)
-    back2_a, back1_a = merge(near2_a, near1_a, far_a)
-    after = (back1_a,)
-    back2_a, back1_a = shifted(back2_a, -2), shifted(back1_a, -1)
-    att, far_b, *state = attend_far(start, places, sent[1], do, half, first_b, 1, after)
+    att, far_b, *state = attend_far(start, places, sent[1], do_b, att, first_b)
     far_b = shifted(far_b, -2)
-    dq, near2_b, near1_b, own_b = attend_near(state, dq, first_b, count_b, (back2_a, back1_a))
-    back2_b, back1_b, total_a = merge(near2_b, near1_b, far_b, own_a, back2_a, back1_a)
-    back2_b, back1_b = shifted(back2_b, -2), shifted(back1_b, -1)
-    grad_k, grad_v = finish(total_a, own_b, back2_b, back1_b)
+    (back1_a,) = merge(near1_kernel, (near1_a,), near1_a, far_a)
+    (back2_a,) = merge(near2_kernel, (near2_a,), near2_a, far_a)
+    back1_a, back2_a = shifted(back1_a, -1), shifted(back2_a, -2)
+    dq, near2_b, near1_b, own_b = attend_near(state, dq, first_b, count_b, ())
+    (back1_b,) = merge(near1_kernel, (near1_b,), near1_b, far_b, back1_a)
+    (back2_b,) = merge(last_near2_kernel, (near2_b,), near2_b, far_b, back1_b)
+    back1_b, back2_b = shifted(back1_b, -1), shifted(back2_b, -2)
+    grad_k, grad_v = finish(own_a, back2_a, back1_a, own_b, back2_b, back1_b)
     return att[None], dq[None], grad_k[None], grad_v[None]
 
 

time: 145 us -> 141 us (0.972)
  starting transfers between devices: 54.4 us -> 51.9 us
  Pallas kernels: 53.2 us -> 51.3 us
  waiting for transfers between devices: 31.4 us -> 32.9 us
    ppermute x10, starting transfers between devices: 35.6 us -> 33.1 us  [shifted(): return lax.ppermute(block, 'ctx', route)]
    pallas_call x4 -> x6, Pallas kernels: 18.9 us -> 17.9 us  [the longest x1 14.7 us: attend_far(): pl.pallas_call(attend_far_kernel, grid=(count,), in_specs=[pl.BlockSpec(s...]
  transfers between devices with their start and end apart: 12 -> 12, of which waited for: 6 -> 8; matrix products, arithmetic and copies ran while one was open for 0% -> 0% of each run, Pallas kernels for 34% -> 34%
where the time goes in v1:
time: 141 us; the launch traced here: 140 us
  starting transfers between devices  51.9 us (37%)
  Pallas kernels  51.3 us (36%)
  waiting for transfers between devices  32.9 us (23%)
  local copies, waits for them, and re-layouts  2.63 us (2%)
    ppermute x10, starting transfers between devices, shifted(): return lax.ppermute(block, 'ctx', route)  33.1 us
    ppermute x10, waiting for transfers between devices, shifted(): return lax.ppermute(block, 'ctx', route)  23.6 us
    pallas_call x1, Pallas kernels, attend(): pl.pallas_call(attend_kernel, grid=(count,), in_specs=[pl.BlockSpec(start...  19.1 us
    all_to_all x2, starting transfers between devices, body(): lax.all_to_all(packed, ('dp', 'ctx'), split_axis=0, concat_axis=0, tiled=...  18.7 us
    pallas_call x1, Pallas kernels, attend_far(): pl.pallas_call(attend_far_kernel, grid=(count,), in_specs=[pl.BlockSpec(s...  14.7 us
    all_to_all x2, waiting for transfers between devices, body(): lax.all_to_all(packed, ('dp', 'ctx'), split_axis=0, concat_axis=0, tiled=...  9.33 us
    pallas_call x1, Pallas kernels, attend_near(): pl.pallas_call(attend_near_kernel, grid=(count,), in_specs=[per_head(a.sh...  6.68 us
    pallas_call x2, Pallas kernels, pack(): pl.pallas_call(first_pack_kernel if later else pack_kernel, grid=(count,)...  6.63 us
  transfers between devices with their start and end apart: 12, of which 8 were waited for; matrix products, arithmetic and copies ran while one was open for 0% of the time, Pallas kernels for 34%

profile of v1, /device:TPU:28, one launch (start us, length us, event | category | flops | bytes accessed | tf_op | source)
XLA Modules:
  0.0 139.8 jit_solution(15438347225580901848)
XLA Ops:
  0.6 3.3 %pack.2 = (bf16[128,2,4608]{2,1,0:T(2,128)(2,1)}, s32[1,8192]{1,0:T(1,128)}, s32[1,256]{1,0:T(1,128)}) custom-call(s32[1,256]{1,0:T(1,128)} %order_ref.3, bf16[256,4096]{1,0:T(8,128)(2,1)} %q_ref.3, bf16[256,512]{1,0:T(8,128)(2,1)} %k_ref.3, bf16[256,512]{1,0:T(8,128)(2,1)} %v_ref.3, s32[1,8192]{1,0:T(1,128)} %doc_ref.1, s32[1,256]{1,0:T(1,128)} %place_ref.1), custom_call_target="tpu_custom_call" | custom-call | tf_op jit(solution)/shard_map/pack/pallas_call | solution.py:78
  4.0 10.3 %all-to-all-start.1 = ((bf16[128,2,4608]{2,1,0:T(2,128)(2,1)}), bf16[128,2,4608]{2,1,0:T(2,128)(2,1)S(1)}, u32[]{:S(2)}, u32[]{:S(2)}) async-start(bf16[128,2,4608]{2,1,0:T(2,128)(2,1)} %get-tuple-element.35), calls=%async_computation.1 | async-start | bytes 4718592 | tf_op jit(solution)/shard_map/all_to_all | solution.py:527
  14.2 3.4 %collective-permute-start.3 = (s32[1,256]{1,0:T(1,128)S(1)}, s32[1,256]{1,0:T(1,128)S(1)}, u32[]{:S(2)}, u32[]{:S(2)}) collective-permute-start(s32[1,256]{1,0:T(1,128)S(1)} %copy-done.3), channel_id=1, source_target_pairs={{0,1},{1,2},{2,3},{3,4},{4,5},{5,6},{6,7},{7,8},{8,9},{9,10},{10,1... | collective-permute-start | bytes 3080 | tf_op jit(solution)/shard_map/ppermute | solution.py:40
  17.7 3.4 %collective-permute-start.2 = (s32[1,256]{1,0:T(1,128)S(1)}, s32[1,256]{1,0:T(1,128)S(1)}, u32[]{:S(2)}, u32[]{:S(2)}) collective-permute-start(s32[1,256]{1,0:T(1,128)S(1)} %copy-done.3), channel_id=1, source_target_pairs={{0,2},{1,3},{2,4},{3,5},{4,6},{5,7},{6,8},{7,9},{8,10},{9,11},{10,... | collective-permute-start | bytes 3080 | tf_op jit(solution)/shard_map/ppermute | solution.py:40
  21.1 5.9 %collective-permute-start.1 = (s32[1,256]{1,0:T(1,128)S(1)}, s32[1,256]{1,0:T(1,128)S(1)}, u32[]{:S(2)}, u32[]{:S(2)}) collective-permute-start(s32[1,256]{1,0:T(1,128)S(1)} %copy-done.3), channel_id=1, source_target_pairs={{0,3},{1,4},{2,5},{3,6},{4,7},{5,8},{6,9},{7,10},{8,11},{9,12},{10... | collective-permute-start | bytes 3080 | tf_op jit(solution)/shard_map/ppermute | solution.py:40
  27.0 4.1 %collective-permute-start = (s32[1,256]{1,0:T(1,128)S(1)}, s32[1,256]{1,0:T(1,128)S(1)}, u32[]{:S(2)}, u32[]{:S(2)}) collective-permute-start(s32[1,256]{1,0:T(1,128)S(1)} %copy-done.3), channel_id=1, source_target_pairs={{0,4},{1,5},{2,6},{3,7},{4,8},{5,9},{6,10},{7,11},{8,12},{9,13},{1... | collective-permute-start | bytes 3080 | tf_op jit(solution)/shard_map/ppermute | solution.py:40
  31.1 0.1 pad_dynamic-slice_fusion
  31.2 0.1 pad_dynamic-slice_fusion.1
  31.3 0.2 convert_reduce_fusion
  31.5 3.3 %pack.3 = bf16[128,2,4608]{2,1,0:T(2,128)(2,1)} custom-call(s32[1,256]{1,0:T(1,128)} %order_ref.3, bf16[256,4096]{1,0:T(8,128)(2,1)} %q_ref.3, bf16[256,512]{1,0:T(8,128)(2,1)} %k_ref.3, bf16[256,512]{1,0:T(8,128)(2,1)} %v_ref.3), custom_call_target="tpu_custom_call" | custom-call | tf_op jit(solution)/shard_map/pack/pallas_call | solution.py:78
  34.8 3.0 %split.1 = (bf16[256,2048]{1,0:T(8,128)(2,1)}, bf16[256,2048]{1,0:T(8,128)(2,1)}) custom-call(bf16[256,4096]{1,0:T(8,128)(2,1)} %bitcast.9, s32[1,8192]{1,0:T(1,128)} %get-tuple-element.32._), custom_call_target="tpu_custom_call" | custom-call | tf_op jit(solution)/shard_map/split/pallas_call | solution.py:458
  37.8 2.6 %collective-permute-done.3 = s32[1,256]{1,0:T(1,128)S(1)} collective-permute-done((s32[1,256]{1,0:T(1,128)S(1)}, s32[1,256]{1,0:T(1,128)S(1)}, u32[]{:S(2)}, u32[]{:S(2)}) %collective-permute-start.3) | collective-permute-done | bytes 1056 | tf_op jit(solution)/shard_map/ppermute | solution.py:40
  40.4 0.5 collective-permute-done.1
  40.9 0.3 collective-permute-done
  41.2 3.0 %all-to-all-done.1.refs_2_ = bf16[128,2,4608]{2,1,0:T(2,128)(2,1)S(1)} async-done(((bf16[128,2,4608]{2,1,0:T(2,128)(2,1)}), bf16[128,2,4608]{2,1,0:T(2,128)(2,1)S(1)}, u32[]{:S(2)}, u32[]{:S(2)}) %all-to-all-start.1) | async-done | bytes 2359328 | tf_op jit(solution)/shard_map/all_to_all | solution.py:527
  44.2 8.5 %all-to-all-start = ((bf16[128,2,4608]{2,1,0:T(2,128)(2,1)}), bf16[128,2,4608]{2,1,0:T(2,128)(2,1)}, u32[]{:S(2)}, u32[]{:S(2)}) async-start(bf16[128,2,4608]{2,1,0:T(2,128)(2,1)} %pack.3), calls=%async_computation | async-start | bytes 4718592 | tf_op jit(solution)/shard_map/all_to_all | solution.py:527
  52.7 1.2 copy-done.1
  53.9 19.1 %attend.1 = (bf16[256,4096]{1,0:T(8,128)(2,1)}, bf16[256,4096]{1,0:T(8,128)(2,1)}, bf16[2,256,512]{2,1,0:T(8,128)(2,1)}, bf16[256,512]{1,0:T(8,128)(2,1)S(1)}, b...) custom-call(s32[1,256]{1,0:T(1,128)S(1)} %bitcast.7, s32[5,256]{1,0:T(8,128)S(1)} %concatenate.3.refs_1_, ...), custom_call_target="tpu_custom_call" | custom-call | flops 32212254720 | bytes 8388608 | tf_op jit(solution)/shard_map/attend/pallas_call | solution.py:303
  73.1 2.9 %collective-permute-start.4 = (bf16[2,256,512]{2,1,0:T(8,128)(2,1)}, bf16[2,256,512]{2,1,0:T(8,128)(2,1)S(1)}, u32[]{:S(2)}, u32[]{:S(2)}) collective-permute-start(bf16[2,256,512]{2,1,0:T(8,128)(2,1)} %get-tuple-element.52), channel_id=1, source_target_pairs={{2,0},{3,1},{4,2},{5,3},{6,4},{7,5},{8,6},{9,7},{10,8},{11,9},{12,... | collective-permute-start | bytes 1572872 | tf_op jit(solution)/shard_map/ppermute | solution.py:40
  76.0 6.4 %all-to-all-done.refs_2_ = bf16[128,2,4608]{2,1,0:T(2,128)(2,1)} async-done(((bf16[128,2,4608]{2,1,0:T(2,128)(2,1)}), bf16[128,2,4608]{2,1,0:T(2,128)(2,1)}, u32[]{:S(2)}, u32[]{:S(2)}) %all-to-all-start) | async-done | bytes 2359328 | tf_op jit(solution)/shard_map/all_to_all | solution.py:527
  82.3 1.2 copy-done
  83.6 14.7 %attend_far.1 = (bf16[256,4096]{1,0:T(8,128)(2,1)}, bf16[2,256,512]{2,1,0:T(8,128)(2,1)S(1)}, bf16[2,8,768,256]{3,2,1,0:T(8,128)(2,1)S(1)}, bf16[2,8,256,128]{3,...) custom-call(s32[1,256]{1,0:T(1,128)S(1)} %bitcast.8, ...), custom_call_target="tpu_custom_call", output_to_operand_aliasing={{0}: (4, {})} | custom-call | flops 19327352832 | bytes 8388608 | tf_op jit(solution)/shard_map/attend_far/pallas_call | solution.py:367
  98.2 2.5 %collective-permute-start.7 = (bf16[2,256,512]{2,1,0:T(8,128)(2,1)S(1)}, bf16[2,256,512]{2,1,0:T(8,128)(2,1)S(1)}, u32[]{:S(2)}, u32[]{:S(2)}) collective-permute-start(bf16[2,256,512]{2,1,0:T(8,128)(2,1)S(1)} %get-tuple-element.56), channel_id=1, source_target_pairs={{2,0},{3,1},{4,2},{5,3},{6,4},{7,5},{8,6},{9,7},{10,8},{11,9},{12,... | collective-permute-start | bytes 1572872 | tf_op jit(solution)/shard_map/ppermute | solution.py:40
  100.8 3.6 %collective-permute-start.6 = (bf16[256,512]{1,0:T(8,128)(2,1)S(1)}, bf16[256,512]{1,0:T(8,128)(2,1)S(1)}, u32[]{:S(2)}, u32[]{:S(2)}) collective-permute-start(bf16[256,512]{1,0:T(8,128)(2,1)S(1)} %merge.5), channel_id=1, source_target_pairs={{1,0},{2,1},{3,2},{4,3},{5,4},{6,5},{7,6},{8,7},{9,8},{10,9},{11,1... | collective-permute-start | bytes 786440 | tf_op jit(solution)/shard_map/ppermute | solution.py:40
  104.4 6.7 %attend_near.1 = (bf16[256,4096]{1,0:T(8,128)(2,1)}, bf16[256,512]{1,0:T(8,128)(2,1)S(1)}, bf16[256,512]{1,0:T(8,128)(2,1)S(1)}, f32[256,512]{1,0:T(8,128)S(1)}) custom-call(bf16[2,8,768,256]{3,2,1,0:T(8,128)(2,1)S(1)} %get-tuple-element.39.refs_0_, bf16[2,8,256,128]{3,2,1,0:T(8,128)(2,1)S(1)} %get-tuple-element.40.refs_1_, ...), custom_call_target="tpu_custom_call", output_to_operand_aliasing={{0}: (9, {})} | custom-call | flops 12884901888 | bytes 8388608 | tf_op jit(solution)/shard_map/attend_near/pallas_call | solution.py:429
  111.2 3.5 %collective-permute-start.5 = (bf16[256,512]{1,0:T(8,128)(2,1)S(1)}, bf16[256,512]{1,0:T(8,128)(2,1)S(1)}, u32[]{:S(2)}, u32[]{:S(2)}) collective-permute-start(bf16[256,512]{1,0:T(8,128)(2,1)S(1)} %merge.4), channel_id=1, source_target_pairs={{2,0},{3,1},{4,2},{5,3},{6,4},{7,5},{8,6},{9,7},{10,8},{11,9},{12,... | collective-permute-start | bytes 786440 | tf_op jit(solution)/shard_map/ppermute | solution.py:40
  114.6 8.1 %collective-permute-done.7.far = bf16[2,256,512]{2,1,0:T(8,128)(2,1)S(1)} collective-permute-done((bf16[2,256,512]{2,1,0:T(8,128)(2,1)S(1)}, bf16[2,256,512]{2,1,0:T(8,128)(2,1)S(1)}, u32[]{:S(2)}, u32[]{:S(2)}) %collective-permute-start.7) | collective-permute-done | bytes 524320 | tf_op jit(solution)/shard_map/ppermute | solution.py:40
  122.8 1.9 %collective-permute-start.8 = (bf16[256,512]{1,0:T(8,128)(2,1)S(1)}, bf16[256,512]{1,0:T(8,128)(2,1)S(1)}, u32[]{:S(2)}, u32[]{:S(2)}) collective-permute-start(bf16[256,512]{1,0:T(8,128)(2,1)S(1)} %merge.7), channel_id=1, source_target_pairs={{2,0},{3,1},{4,2},{5,3},{6,4},{7,5},{8,6},{9,7},{10,8},{11,9},{12,... | collective-permute-start | bytes 786440 | tf_op jit(solution)/shard_map/ppermute | solution.py:40
  124.8 1.9 %collective-permute-start.9 = (bf16[256,512]{1,0:T(8,128)(2,1)S(1)}, bf16[256,512]{1,0:T(8,128)(2,1)S(1)}, u32[]{:S(2)}, u32[]{:S(2)}) collective-permute-start(bf16[256,512]{1,0:T(8,128)(2,1)S(1)} %merge.6._), channel_id=1, source_target_pairs={{1,0},{2,1},{3,2},{4,3},{5,4},{6,5},{7,6},{8,7},{9,8},{10,9},{11,1... | collective-permute-start | bytes 786440 | tf_op jit(solution)/shard_map/ppermute | solution.py:40
  126.7 0.3 collective-permute-done.5.back2_a
  127.0 11.8 %collective-permute-done.8.back2_b = bf16[256,512]{1,0:T(8,128)(2,1)S(1)} collective-permute-done((bf16[256,512]{1,0:T(8,128)(2,1)S(1)}, bf16[256,512]{1,0:T(8,128)(2,1)S(1)}, u32[]{:S(2)}, u32[]{:S(2)}) %collective-permute-start.8) | collective-permute-done | bytes 262176 | tf_op jit(solution)/shard_map/ppermute | solution.py:40
  138.8 1.0 finish.1
  (15 shorter events, 0.3 us)
Async XLA Ops:
  4.0 10.3 %copy-start.3 = (s32[1,256]{1,0:T(1,128)S(1)}, s32[1,256]{1,0:T(1,128)}, u32[]{:S(2)}) copy-start(s32[1,256]{1,0:T(1,128)} %get-tuple-element.33) | copy-start | bytes 3076
  4.0 27.1 %copy-start.2 = (s32[1,8192]{1,0:T(1,128)S(1)}, s32[1,8192]{1,0:T(1,128)}, u32[]{:S(2)}) copy-start(s32[1,8192]{1,0:T(1,128)} %get-tuple-element.32._) | copy-start | bytes 98308
  4.0 40.2 %all-to-all-start.1 = ((bf16[128,2,4608]{2,1,0:T(2,128)(2,1)}), bf16[128,2,4608]{2,1,0:T(2,128)(2,1)S(1)}, u32[]{:S(2)}, u32[]{:S(2)}) async-start(bf16[128,2,4608]{2,1,0:T(2,128)(2,1)} %get-tuple-element.35), calls=%async_computation.1 | async-start | bytes 4718592 | tf_op jit(solution)/shard_map/all_to_all | solution.py:527
  14.2 26.2 %collective-permute-start.3 = (s32[1,256]{1,0:T(1,128)S(1)}, s32[1,256]{1,0:T(1,128)S(1)}, u32[]{:S(2)}, u32[]{:S(2)}) collective-permute-start(s32[1,256]{1,0:T(1,128)S(1)} %copy-done.3), channel_id=1, source_target_pairs={{0,1},{1,2},{2,3},{3,4},{4,5},{5,6},{6,7},{7,8},{8,9},{9,10},{10,1... | collective-permute-start | bytes 3080 | tf_op jit(solution)/shard_map/ppermute | solution.py:40
  17.7 22.8 %collective-permute-start.2 = (s32[1,256]{1,0:T(1,128)S(1)}, s32[1,256]{1,0:T(1,128)S(1)}, u32[]{:S(2)}, u32[]{:S(2)}) collective-permute-start(s32[1,256]{1,0:T(1,128)S(1)} %copy-done.3), channel_id=1, source_target_pairs={{0,2},{1,3},{2,4},{3,5},{4,6},{5,7},{6,8},{7,9},{8,10},{9,11},{10,... | collective-permute-start | bytes 3080 | tf_op jit(solution)/shard_map/ppermute | solution.py:40
  21.1 19.8 %collective-permute-start.1 = (s32[1,256]{1,0:T(1,128)S(1)}, s32[1,256]{1,0:T(1,128)S(1)}, u32[]{:S(2)}, u32[]{:S(2)}) collective-permute-start(s32[1,256]{1,0:T(1,128)S(1)} %copy-done.3), channel_id=1, source_target_pairs={{0,3},{1,4},{2,5},{3,6},{4,7},{5,8},{6,9},{7,10},{8,11},{9,12},{10... | collective-permute-start | bytes 3080 | tf_op jit(solution)/shard_map/ppermute | solution.py:40
  27.0 14.2 %collective-permute-start = (s32[1,256]{1,0:T(1,128)S(1)}, s32[1,256]{1,0:T(1,128)S(1)}, u32[]{:S(2)}, u32[]{:S(2)}) collective-permute-start(s32[1,256]{1,0:T(1,128)S(1)} %copy-done.3), channel_id=1, source_target_pairs={{0,4},{1,5},{2,6},{3,7},{4,8},{5,9},{6,10},{7,11},{8,12},{9,13},{1... | collective-permute-start | bytes 3080 | tf_op jit(solution)/shard_map/ppermute | solution.py:40
  44.2 38.1 %all-to-all-start = ((bf16[128,2,4608]{2,1,0:T(2,128)(2,1)}), bf16[128,2,4608]{2,1,0:T(2,128)(2,1)}, u32[]{:S(2)}, u32[]{:S(2)}) async-start(bf16[128,2,4608]{2,1,0:T(2,128)(2,1)} %pack.3), calls=%async_computation | async-start | bytes 4718592 | tf_op jit(solution)/shard_map/all_to_all | solution.py:527
  52.7 1.2 copy-start.1
  73.1 27.7 %collective-permute-start.4 = (bf16[2,256,512]{2,1,0:T(8,128)(2,1)}, bf16[2,256,512]{2,1,0:T(8,128)(2,1)S(1)}, u32[]{:S(2)}, u32[]{:S(2)}) collective-permute-start(bf16[2,256,512]{2,1,0:T(8,128)(2,1)} %get-tuple-element.52), channel_id=1, source_target_pairs={{2,0},{3,1},{4,2},{5,3},{6,4},{7,5},{8,6},{9,7},{10,8},{11,9},{12,... | collective-permute-start | bytes 1572872 | tf_op jit(solution)/shard_map/ppermute | solution.py:40
  82.3 1.2 copy-start
  98.2 24.5 %collective-permute-start.7 = (bf16[2,256,512]{2,1,0:T(8,128)(2,1)S(1)}, bf16[2,256,512]{2,1,0:T(8,128)(2,1)S(1)}, u32[]{:S(2)}, u32[]{:S(2)}) collective-permute-start(bf16[2,256,512]{2,1,0:T(8,128)(2,1)S(1)} %get-tuple-element.56), channel_id=1, source_target_pairs={{2,0},{3,1},{4,2},{5,3},{6,4},{7,5},{8,6},{9,7},{10,8},{11,9},{12,... | collective-permute-start | bytes 1572872 | tf_op jit(solution)/shard_map/ppermute | solution.py:40
  100.8 21.9 %collective-permute-start.6 = (bf16[256,512]{1,0:T(8,128)(2,1)S(1)}, bf16[256,512]{1,0:T(8,128)(2,1)S(1)}, u32[]{:S(2)}, u32[]{:S(2)}) collective-permute-start(bf16[256,512]{1,0:T(8,128)(2,1)S(1)} %merge.5), channel_id=1, source_target_pairs={{1,0},{2,1},{3,2},{4,3},{5,4},{6,5},{7,6},{8,7},{9,8},{10,9},{11,1... | collective-permute-start | bytes 786440 | tf_op jit(solution)/shard_map/ppermute | solution.py:40
  111.2 15.9 %collective-permute-start.5 = (bf16[256,512]{1,0:T(8,128)(2,1)S(1)}, bf16[256,512]{1,0:T(8,128)(2,1)S(1)}, u32[]{:S(2)}, u32[]{:S(2)}) collective-permute-start(bf16[256,512]{1,0:T(8,128)(2,1)S(1)} %merge.4), channel_id=1, source_target_pairs={{2,0},{3,1},{4,2},{5,3},{6,4},{7,5},{8,6},{9,7},{10,8},{11,9},{12,... | collective-permute-start | bytes 786440 | tf_op jit(solution)/shard_map/ppermute | solution.py:40
  122.8 16.0 %collective-permute-start.8 = (bf16[256,512]{1,0:T(8,128)(2,1)S(1)}, bf16[256,512]{1,0:T(8,128)(2,1)S(1)}, u32[]{:S(2)}, u32[]{:S(2)}) collective-permute-start(bf16[256,512]{1,0:T(8,128)(2,1)S(1)} %merge.7), channel_id=1, source_target_pairs={{2,0},{3,1},{4,2},{5,3},{6,4},{7,5},{8,6},{9,7},{10,8},{11,9},{12,... | collective-permute-start | bytes 786440 | tf_op jit(solution)/shard_map/ppermute | solution.py:40
  124.8 14.1 %collective-permute-start.9 = (bf16[256,512]{1,0:T(8,128)(2,1)S(1)}, bf16[256,512]{1,0:T(8,128)(2,1)S(1)}, u32[]{:S(2)}, u32[]{:S(2)}) collective-permute-start(bf16[256,512]{1,0:T(8,128)(2,1)S(1)} %merge.6._), channel_id=1, source_target_pairs={{1,0},{2,1},{3,2},{4,3},{5,4},{6,5},{7,6},{8,7},{9,8},{10,9},{11,1... | collective-permute-start | bytes 786440 | tf_op jit(solution)/shard_map/ppermute | solution.py:40

commit v2 on v1

--- a/solution.py
+++ b/solution.py
@@ -28,6 +28,7 @@
 ATTEND_LIMIT = 32 * 1024 * 1024
 FAR_LIMIT = 32 * 1024 * 1024
 SMALL_LIMIT = 8 * 1024 * 1024
+SPLIT_LIMIT = 16 * 1024 * 1024
 
 
 def dot(a, b):
@@ -461,7 +462,7 @@
         in_specs=[pl.BlockSpec(do.shape, lambda h: (0, 0)), pl.BlockSpec(memory_space=pl.ANY)],
         out_specs=[pl.BlockSpec((tok, n * QCOLS), lambda h: (0, 0)) for n in counts],
         out_shape=[jax.ShapeDtypeStruct((tok, n * QCOLS), jnp.bfloat16) for n in counts],
-        compiler_params=pltpu.CompilerParams(vmem_limit_bytes=VMEM_LIMIT),
+        compiler_params=pltpu.CompilerParams(vmem_limit_bytes=SPLIT_LIMIT),
         name="split",
     )(do, after)
 

time: 141 us -> 141 us (level)
  local copies, waits for them, and re-layouts: 2.63 us -> 6.18 us
  Pallas kernels: 51.3 us -> 48.5 us
    unnamed x8 -> x14, local copies, waits for them, and re-layouts: 2.45 us -> 6 us
    pallas_call x1, Pallas kernels: 3 us -> 0.14 us  [split(): pl.pallas_call(split_kernel, grid=(1,), in_specs=[pl.BlockSpec(do.shape,...]
  transfers between devices with their start and end apart: 12 -> 12, of which waited for: 8 -> 8; matrix products, arithmetic and copies ran while one was open for 0% -> 0% of each run, Pallas kernels for 34% -> 32%
where the time goes in v2:
time: 141 us; the launch traced here: 140 us
  starting transfers between devices  51.9 us (37%)
  Pallas kernels  48.5 us (34%)
  waiting for transfers between devices  32.2 us (23%)
  local copies, waits for them, and re-layouts  6.18 us (4%)
    ppermute x10, starting transfers between devices, shifted(): return lax.ppermute(block, 'ctx', route)  33.1 us
    ppermute x10, waiting for transfers between devices, shifted(): return lax.ppermute(block, 'ctx', route)  22.9 us
    pallas_call x1, Pallas kernels, attend(): pl.pallas_call(attend_kernel, grid=(count,), in_specs=[pl.BlockSpec(start...  19.1 us
    all_to_all x2, starting transfers between devices, body(): lax.all_to_all(packed, ('dp', 'ctx'), split_axis=0, concat_axis=0, tiled=...  18.7 us
    pallas_call x1, Pallas kernels, attend_far(): pl.pallas_call(attend_far_kernel, grid=(count,), in_specs=[pl.BlockSpec(s...  14.7 us
    all_to_all x2, waiting for transfers between devices, body(): lax.all_to_all(packed, ('dp', 'ctx'), split_axis=0, concat_axis=0, tiled=...  9.31 us
    pallas_call x1, Pallas kernels, attend_near(): pl.pallas_call(attend_near_kernel, grid=(count,), in_specs=[per_head(a.sh...  6.68 us
    pallas_call x2, Pallas kernels, pack(): pl.pallas_call(first_pack_kernel if later else pack_kernel, grid=(count,)...  6.65 us
  transfers between devices with their start and end apart: 12, of which 8 were waited for; matrix products, arithmetic and copies ran while one was open for 0% of the time, Pallas kernels for 32%

profile of v2, /device:TPU:28, one launch (start us, length us, event | category | flops | bytes accessed | tf_op | source)
XLA Modules:
  0.0 139.8 jit_solution(13735526306627023243)
XLA Ops:
  0.6 3.4 %pack.2 = (bf16[128,2,4608]{2,1,0:T(2,128)(2,1)}, s32[1,8192]{1,0:T(1,128)}, s32[1,256]{1,0:T(1,128)}) custom-call(s32[1,256]{1,0:T(1,128)} %order_ref.3, bf16[256,4096]{1,0:T(8,128)(2,1)} %q_ref.3, bf16[256,512]{1,0:T(8,128)(2,1)} %k_ref.3, bf16[256,512]{1,0:T(8,128)(2,1)} %v_ref.3, s32[1,8192]{1,0:T(1,128)} %doc_ref.1, s32[1,256]{1,0:T(1,128)} %place_ref.1), custom_call_target="tpu_custom_call" | custom-call | tf_op jit(solution)/shard_map/pack/pallas_call | solution.py:79
  4.0 10.3 %all-to-all-start.1 = ((bf16[128,2,4608]{2,1,0:T(2,128)(2,1)}), bf16[128,2,4608]{2,1,0:T(2,128)(2,1)S(1)}, u32[]{:S(2)}, u32[]{:S(2)}) async-start(bf16[128,2,4608]{2,1,0:T(2,128)(2,1)} %get-tuple-element.35), calls=%async_computation.1 | async-start | bytes 4718592 | tf_op jit(solution)/shard_map/all_to_all | solution.py:528
  14.3 3.4 %collective-permute-start.3 = (s32[1,256]{1,0:T(1,128)S(1)}, s32[1,256]{1,0:T(1,128)S(1)}, u32[]{:S(2)}, u32[]{:S(2)}) collective-permute-start(s32[1,256]{1,0:T(1,128)S(1)} %copy-done.6), channel_id=1, source_target_pairs={{0,1},{1,2},{2,3},{3,4},{4,5},{5,6},{6,7},{7,8},{8,9},{9,10},{10,1... | collective-permute-start | bytes 3080 | tf_op jit(solution)/shard_map/ppermute | solution.py:41
  17.7 3.4 %collective-permute-start.2 = (s32[1,256]{1,0:T(1,128)S(1)}, s32[1,256]{1,0:T(1,128)S(1)}, u32[]{:S(2)}, u32[]{:S(2)}) collective-permute-start(s32[1,256]{1,0:T(1,128)S(1)} %copy-done.6), channel_id=1, source_target_pairs={{0,2},{1,3},{2,4},{3,5},{4,6},{5,7},{6,8},{7,9},{8,10},{9,11},{10,... | collective-permute-start | bytes 3080 | tf_op jit(solution)/shard_map/ppermute | solution.py:41
  21.1 5.9 %collective-permute-start.1 = (s32[1,256]{1,0:T(1,128)S(1)}, s32[1,256]{1,0:T(1,128)S(1)}, u32[]{:S(2)}, u32[]{:S(2)}) collective-permute-start(s32[1,256]{1,0:T(1,128)S(1)} %copy-done.6), channel_id=1, source_target_pairs={{0,3},{1,4},{2,5},{3,6},{4,7},{5,8},{6,9},{7,10},{8,11},{9,12},{10... | collective-permute-start | bytes 3080 | tf_op jit(solution)/shard_map/ppermute | solution.py:41
  27.0 4.1 %collective-permute-start = (s32[1,256]{1,0:T(1,128)S(1)}, s32[1,256]{1,0:T(1,128)S(1)}, u32[]{:S(2)}, u32[]{:S(2)}) collective-permute-start(s32[1,256]{1,0:T(1,128)S(1)} %copy-done.6), channel_id=1, source_target_pairs={{0,4},{1,5},{2,6},{3,7},{4,8},{5,9},{6,10},{7,11},{8,12},{9,13},{1... | collective-permute-start | bytes 3080 | tf_op jit(solution)/shard_map/ppermute | solution.py:41
  31.3 0.2 convert_reduce_fusion
  31.5 3.3 %pack.3 = bf16[128,2,4608]{2,1,0:T(2,128)(2,1)} custom-call(s32[1,256]{1,0:T(1,128)} %order_ref.3, bf16[256,4096]{1,0:T(8,128)(2,1)} %q_ref.3, bf16[256,512]{1,0:T(8,128)(2,1)} %k_ref.3, bf16[256,512]{1,0:T(8,128)(2,1)} %v_ref.3), custom_call_target="tpu_custom_call" | custom-call | tf_op jit(solution)/shard_map/pack/pallas_call | solution.py:79
  34.8 1.6 %copy-done = bf16[1,256,4096]{2,1,0:T(8,128)(2,1)S(1)} copy-done((bf16[1,256,4096]{2,1,0:T(8,128)(2,1)S(1)}, bf16[1,256,4096]{2,1,0:T(8,128)(2,1)}, u32[]{:S(2)}) %copy-start) | copy-done | bytes 2097176
  36.6 1.0 copy-done.2
  37.6 1.0 copy-done.4
  38.5 1.9 %collective-permute-done.3 = s32[1,256]{1,0:T(1,128)S(1)} collective-permute-done((s32[1,256]{1,0:T(1,128)S(1)}, s32[1,256]{1,0:T(1,128)S(1)}, u32[]{:S(2)}, u32[]{:S(2)}) %collective-permute-start.3) | collective-permute-done | bytes 1056 | tf_op jit(solution)/shard_map/ppermute | solution.py:41
  40.4 0.5 collective-permute-done.1
  40.9 0.3 collective-permute-done
  41.2 3.0 %all-to-all-done.1.refs_2_ = bf16[128,2,4608]{2,1,0:T(2,128)(2,1)S(1)} async-done(((bf16[128,2,4608]{2,1,0:T(2,128)(2,1)}), bf16[128,2,4608]{2,1,0:T(2,128)(2,1)S(1)}, u32[]{:S(2)}, u32[]{:S(2)}) %all-to-all-start.1) | async-done | bytes 2359328 | tf_op jit(solution)/shard_map/all_to_all | solution.py:528
  44.2 8.5 %all-to-all-start = ((bf16[128,2,4608]{2,1,0:T(2,128)(2,1)}), bf16[128,2,4608]{2,1,0:T(2,128)(2,1)}, u32[]{:S(2)}, u32[]{:S(2)}) async-start(bf16[128,2,4608]{2,1,0:T(2,128)(2,1)} %pack.3), calls=%async_computation | async-start | bytes 4718592 | tf_op jit(solution)/shard_map/all_to_all | solution.py:528
  52.7 1.2 copy-done.5
  53.9 19.1 %attend.1 = (bf16[256,4096]{1,0:T(8,128)(2,1)}, bf16[256,4096]{1,0:T(8,128)(2,1)}, bf16[2,256,512]{2,1,0:T(8,128)(2,1)}, bf16[256,512]{1,0:T(8,128)(2,1)S(1)}, b...) custom-call(s32[1,256]{1,0:T(1,128)S(1)} %bitcast.10, s32[5,256]{1,0:T(8,128)S(1)} %concatenate.3.refs_1_, ...), custom_call_target="tpu_custom_call" | custom-call | flops 32212254720 | bytes 8388608 | tf_op jit(solution)/shard_map/attend/pallas_call | solution.py:304
  73.1 2.9 %collective-permute-start.4 = (bf16[2,256,512]{2,1,0:T(8,128)(2,1)}, bf16[2,256,512]{2,1,0:T(8,128)(2,1)S(1)}, u32[]{:S(2)}, u32[]{:S(2)}) collective-permute-start(bf16[2,256,512]{2,1,0:T(8,128)(2,1)} %get-tuple-element.52), channel_id=1, source_target_pairs={{2,0},{3,1},{4,2},{5,3},{6,4},{7,5},{8,6},{9,7},{10,8},{11,9},{12,... | collective-permute-start | bytes 1572872 | tf_op jit(solution)/shard_map/ppermute | solution.py:41
  76.0 6.3 %all-to-all-done.refs_2_ = bf16[128,2,4608]{2,1,0:T(2,128)(2,1)} async-done(((bf16[128,2,4608]{2,1,0:T(2,128)(2,1)}), bf16[128,2,4608]{2,1,0:T(2,128)(2,1)}, u32[]{:S(2)}, u32[]{:S(2)}) %all-to-all-start) | async-done | bytes 2359328 | tf_op jit(solution)/shard_map/all_to_all | solution.py:528
  82.3 1.2 copy-done.3
  83.6 14.7 %attend_far.1 = (bf16[256,4096]{1,0:T(8,128)(2,1)}, bf16[2,256,512]{2,1,0:T(8,128)(2,1)S(1)}, bf16[2,8,768,256]{3,2,1,0:T(8,128)(2,1)S(1)}, bf16[2,8,256,128]{3,...) custom-call(s32[1,256]{1,0:T(1,128)S(1)} %bitcast.11, ...), custom_call_target="tpu_custom_call", output_to_operand_aliasing={{0}: (4, {})} | custom-call | flops 19327352832 | bytes 8388608 | tf_op jit(solution)/shard_map/attend_far/pallas_call | solution.py:368
  98.3 2.5 %collective-permute-start.7 = (bf16[2,256,512]{2,1,0:T(8,128)(2,1)S(1)}, bf16[2,256,512]{2,1,0:T(8,128)(2,1)S(1)}, u32[]{:S(2)}, u32[]{:S(2)}) collective-permute-start(bf16[2,256,512]{2,1,0:T(8,128)(2,1)S(1)} %get-tuple-element.56), channel_id=1, source_target_pairs={{2,0},{3,1},{4,2},{5,3},{6,4},{7,5},{8,6},{9,7},{10,8},{11,9},{12,... | collective-permute-start | bytes 1572872 | tf_op jit(solution)/shard_map/ppermute | solution.py:41
  100.8 3.6 %collective-permute-start.6 = (bf16[256,512]{1,0:T(8,128)(2,1)S(1)}, bf16[256,512]{1,0:T(8,128)(2,1)S(1)}, u32[]{:S(2)}, u32[]{:S(2)}) collective-permute-start(bf16[256,512]{1,0:T(8,128)(2,1)S(1)} %merge.5), channel_id=1, source_target_pairs={{1,0},{2,1},{3,2},{4,3},{5,4},{6,5},{7,6},{8,7},{9,8},{10,9},{11,1... | collective-permute-start | bytes 786440 | tf_op jit(solution)/shard_map/ppermute | solution.py:41
  104.4 6.7 %attend_near.1 = (bf16[256,4096]{1,0:T(8,128)(2,1)}, bf16[256,512]{1,0:T(8,128)(2,1)S(1)}, bf16[256,512]{1,0:T(8,128)(2,1)S(1)}, f32[256,512]{1,0:T(8,128)S(1)}) custom-call(bf16[2,8,768,256]{3,2,1,0:T(8,128)(2,1)S(1)} %get-tuple-element.39.refs_0_, bf16[2,8,256,128]{3,2,1,0:T(8,128)(2,1)S(1)} %get-tuple-element.40.refs_1_, ...), custom_call_target="tpu_custom_call", output_to_operand_aliasing={{0}: (9, {})} | custom-call | flops 12884901888 | bytes 8388608 | tf_op jit(solution)/shard_map/attend_near/pallas_call | solution.py:430
  111.2 3.5 %collective-permute-start.5 = (bf16[256,512]{1,0:T(8,128)(2,1)S(1)}, bf16[256,512]{1,0:T(8,128)(2,1)S(1)}, u32[]{:S(2)}, u32[]{:S(2)}) collective-permute-start(bf16[256,512]{1,0:T(8,128)(2,1)S(1)} %merge.4), channel_id=1, source_target_pairs={{2,0},{3,1},{4,2},{5,3},{6,4},{7,5},{8,6},{9,7},{10,8},{11,9},{12,... | collective-permute-start | bytes 786440 | tf_op jit(solution)/shard_map/ppermute | solution.py:41
  114.7 8.1 %collective-permute-done.7.far = bf16[2,256,512]{2,1,0:T(8,128)(2,1)S(1)} collective-permute-done((bf16[2,256,512]{2,1,0:T(8,128)(2,1)S(1)}, bf16[2,256,512]{2,1,0:T(8,128)(2,1)S(1)}, u32[]{:S(2)}, u32[]{:S(2)}) %collective-permute-start.7) | collective-permute-done | bytes 524320 | tf_op jit(solution)/shard_map/ppermute | solution.py:41
  122.9 1.9 %collective-permute-start.8 = (bf16[256,512]{1,0:T(8,128)(2,1)S(1)}, bf16[256,512]{1,0:T(8,128)(2,1)S(1)}, u32[]{:S(2)}, u32[]{:S(2)}) collective-permute-start(bf16[256,512]{1,0:T(8,128)(2,1)S(1)} %merge.7), channel_id=1, source_target_pairs={{2,0},{3,1},{4,2},{5,3},{6,4},{7,5},{8,6},{9,7},{10,8},{11,9},{12,... | collective-permute-start | bytes 786440 | tf_op jit(solution)/shard_map/ppermute | solution.py:41
  124.8 1.9 %collective-permute-start.9 = (bf16[256,512]{1,0:T(8,128)(2,1)S(1)}, bf16[256,512]{1,0:T(8,128)(2,1)S(1)}, u32[]{:S(2)}, u32[]{:S(2)}) collective-permute-start(bf16[256,512]{1,0:T(8,128)(2,1)S(1)} %merge.6._), channel_id=1, source_target_pairs={{1,0},{2,1},{3,2},{4,3},{5,4},{6,5},{7,6},{8,7},{9,8},{10,9},{11,1... | collective-permute-start | bytes 786440 | tf_op jit(solution)/shard_map/ppermute | solution.py:41
  126.7 0.3 collective-permute-done.5.back2_a
  127.0 11.8 %collective-permute-done.8.back2_b = bf16[256,512]{1,0:T(8,128)(2,1)S(1)} collective-permute-done((bf16[256,512]{1,0:T(8,128)(2,1)S(1)}, bf16[256,512]{1,0:T(8,128)(2,1)S(1)}, u32[]{:S(2)}, u32[]{:S(2)}) %collective-permute-start.8) | collective-permute-done | bytes 262176 | tf_op jit(solution)/shard_map/ppermute | solution.py:41
  138.9 1.0 finish.1
  (21 shorter events, 0.6 us)
Async XLA Ops:
  4.0 10.3 %copy-start.6 = (s32[1,256]{1,0:T(1,128)S(1)}, s32[1,256]{1,0:T(1,128)}, u32[]{:S(2)}) copy-start(s32[1,256]{1,0:T(1,128)} %get-tuple-element.33) | copy-start | bytes 3076
  4.0 27.1 %copy-start.1 = (s32[1,8192]{1,0:T(1,128)S(1)}, s32[1,8192]{1,0:T(1,128)}, u32[]{:S(2)}) copy-start(s32[1,8192]{1,0:T(1,128)} %get-tuple-element.32._) | copy-start | bytes 98308
  4.0 40.2 %all-to-all-start.1 = ((bf16[128,2,4608]{2,1,0:T(2,128)(2,1)}), bf16[128,2,4608]{2,1,0:T(2,128)(2,1)S(1)}, u32[]{:S(2)}, u32[]{:S(2)}) async-start(bf16[128,2,4608]{2,1,0:T(2,128)(2,1)} %get-tuple-element.35), calls=%async_computation.1 | async-start | bytes 4718592 | tf_op jit(solution)/shard_map/all_to_all | solution.py:528
  14.3 26.2 %collective-permute-start.3 = (s32[1,256]{1,0:T(1,128)S(1)}, s32[1,256]{1,0:T(1,128)S(1)}, u32[]{:S(2)}, u32[]{:S(2)}) collective-permute-start(s32[1,256]{1,0:T(1,128)S(1)} %copy-done.6), channel_id=1, source_target_pairs={{0,1},{1,2},{2,3},{3,4},{4,5},{5,6},{6,7},{7,8},{8,9},{9,10},{10,1... | collective-permute-start | bytes 3080 | tf_op jit(solution)/shard_map/ppermute | solution.py:41
  17.7 22.8 %collective-permute-start.2 = (s32[1,256]{1,0:T(1,128)S(1)}, s32[1,256]{1,0:T(1,128)S(1)}, u32[]{:S(2)}, u32[]{:S(2)}) collective-permute-start(s32[1,256]{1,0:T(1,128)S(1)} %copy-done.6), channel_id=1, source_target_pairs={{0,2},{1,3},{2,4},{3,5},{4,6},{5,7},{6,8},{7,9},{8,10},{9,11},{10,... | collective-permute-start | bytes 3080 | tf_op jit(solution)/shard_map/ppermute | solution.py:41
  21.1 19.8 %collective-permute-start.1 = (s32[1,256]{1,0:T(1,128)S(1)}, s32[1,256]{1,0:T(1,128)S(1)}, u32[]{:S(2)}, u32[]{:S(2)}) collective-permute-start(s32[1,256]{1,0:T(1,128)S(1)} %copy-done.6), channel_id=1, source_target_pairs={{0,3},{1,4},{2,5},{3,6},{4,7},{5,8},{6,9},{7,10},{8,11},{9,12},{10... | collective-permute-start | bytes 3080 | tf_op jit(solution)/shard_map/ppermute | solution.py:41
  27.0 14.2 %collective-permute-start = (s32[1,256]{1,0:T(1,128)S(1)}, s32[1,256]{1,0:T(1,128)S(1)}, u32[]{:S(2)}, u32[]{:S(2)}) collective-permute-start(s32[1,256]{1,0:T(1,128)S(1)} %copy-done.6), channel_id=1, source_target_pairs={{0,4},{1,5},{2,6},{3,7},{4,8},{5,9},{6,10},{7,11},{8,12},{9,13},{1... | collective-permute-start | bytes 3080 | tf_op jit(solution)/shard_map/ppermute | solution.py:41
  34.8 1.6 %copy-start = (bf16[1,256,4096]{2,1,0:T(8,128)(2,1)S(1)}, bf16[1,256,4096]{2,1,0:T(8,128)(2,1)}, u32[]{:S(2)}) copy-start(bf16[1,256,4096]{2,1,0:T(8,128)(2,1)} %param.10) | copy-start | bytes 6291460
  36.6 1.0 copy-start.2
  37.6 1.0 copy-start.4
  44.2 38.1 %all-to-all-start = ((bf16[128,2,4608]{2,1,0:T(2,128)(2,1)}), bf16[128,2,4608]{2,1,0:T(2,128)(2,1)}, u32[]{:S(2)}, u32[]{:S(2)}) async-start(bf16[128,2,4608]{2,1,0:T(2,128)(2,1)} %pack.3), calls=%async_computation | async-start | bytes 4718592 | tf_op jit(solution)/shard_map/all_to_all | solution.py:528
  52.7 1.2 copy-start.5
  73.1 27.7 %collective-permute-start.4 = (bf16[2,256,512]{2,1,0:T(8,128)(2,1)}, bf16[2,256,512]{2,1,0:T(8,128)(2,1)S(1)}, u32[]{:S(2)}, u32[]{:S(2)}) collective-permute-start(bf16[2,256,512]{2,1,0:T(8,128)(2,1)} %get-tuple-element.52), channel_id=1, source_target_pairs={{2,0},{3,1},{4,2},{5,3},{6,4},{7,5},{8,6},{9,7},{10,8},{11,9},{12,... | collective-permute-start | bytes 1572872 | tf_op jit(solution)/shard_map/ppermute | solution.py:41
  82.3 1.2 copy-start.3
  98.3 24.5 %collective-permute-start.7 = (bf16[2,256,512]{2,1,0:T(8,128)(2,1)S(1)}, bf16[2,256,512]{2,1,0:T(8,128)(2,1)S(1)}, u32[]{:S(2)}, u32[]{:S(2)}) collective-permute-start(bf16[2,256,512]{2,1,0:T(8,128)(2,1)S(1)} %get-tuple-element.56), channel_id=1, source_target_pairs={{2,0},{3,1},{4,2},{5,3},{6,4},{7,5},{8,6},{9,7},{10,8},{11,9},{12,... | collective-permute-start | bytes 1572872 | tf_op jit(solution)/shard_map/ppermute | solution.py:41
  100.8 21.9 %collective-permute-start.6 = (bf16[256,512]{1,0:T(8,128)(2,1)S(1)}, bf16[256,512]{1,0:T(8,128)(2,1)S(1)}, u32[]{:S(2)}, u32[]{:S(2)}) collective-permute-start(bf16[256,512]{1,0:T(8,128)(2,1)S(1)} %merge.5), channel_id=1, source_target_pairs={{1,0},{2,1},{3,2},{4,3},{5,4},{6,5},{7,6},{8,7},{9,8},{10,9},{11,1... | collective-permute-start | bytes 786440 | tf_op jit(solution)/shard_map/ppermute | solution.py:41
  111.2 15.9 %collective-permute-start.5 = (bf16[256,512]{1,0:T(8,128)(2,1)S(1)}, bf16[256,512]{1,0:T(8,128)(2,1)S(1)}, u32[]{:S(2)}, u32[]{:S(2)}) collective-permute-start(bf16[256,512]{1,0:T(8,128)(2,1)S(1)} %merge.4), channel_id=1, source_target_pairs={{2,0},{3,1},{4,2},{5,3},{6,4},{7,5},{8,6},{9,7},{10,8},{11,9},{12,... | collective-permute-start | bytes 786440 | tf_op jit(solution)/shard_map/ppermute | solution.py:41
  122.9 16.0 %collective-permute-start.8 = (bf16[256,512]{1,0:T(8,128)(2,1)S(1)}, bf16[256,512]{1,0:T(8,128)(2,1)S(1)}, u32[]{:S(2)}, u32[]{:S(2)}) collective-permute-start(bf16[256,512]{1,0:T(8,128)(2,1)S(1)} %merge.7), channel_id=1, source_target_pairs={{2,0},{3,1},{4,2},{5,3},{6,4},{7,5},{8,6},{9,7},{10,8},{11,9},{12,... | collective-permute-start | bytes 786440 | tf_op jit(solution)/shard_map/ppermute | solution.py:41
  124.8 14.1 %collective-permute-start.9 = (bf16[256,512]{1,0:T(8,128)(2,1)S(1)}, bf16[256,512]{1,0:T(8,128)(2,1)S(1)}, u32[]{:S(2)}, u32[]{:S(2)}) collective-permute-start(bf16[256,512]{1,0:T(8,128)(2,1)S(1)} %merge.6._), channel_id=1, source_target_pairs={{1,0},{2,1},{3,2},{4,3},{5,4},{6,5},{7,6},{8,7},{9,8},{10,9},{11,1... | collective-permute-start | bytes 786440 | tf_op jit(solution)/shard_map/ppermute | solution.py:41
